TPU v7x, 32 devices: a whole 2x2x4 slice. The times are simulated.
32 devices in a mesh: ifg: 8 (over z, x), grp: 4 (over y, core).
Axes of the slice: x: 2, y: 2, z: 4, core: 2. Of those that a mesh axis runs over, the one named last changes fastest.
Arguments:
- phases: bfloat16 [1024, 4, 32768], P('ifg', 'grp'), may hold values from -6 to 6
- date_pairs: int32 [2, 1024], replicated, may hold values from 0 to 199, as said below
- pair_counts: int32 [16], replicated, may hold values from 128 to 1024, as said below
- group_ids: int32 [4, 128], P(None, 'ifg'), may hold values from 0 to 15, as said below
Outputs:
- series: float32 [4, 200, 32768], P('grp', None, 'ifg')
Inputs may be any that keep to these rules, and one draw needn't show every extreme that they name: date_pairs[0, k] < date_pairs[1, k]; the baseline date_pairs[1, k] - date_pairs[0, k] lies in 1 to 25 and never falls as k grows. `pair_counts`: each count is 128 times a power of two; some class has all 1024 interferograms and some has 128. `group_ids`: constant over each aligned run of 8 blocks of a sub-strip.
All inputs are finite; a program needn't handle non-finite values.
Results may differ from a plain program's by a relative error of at most 0.0003.
Values may be sent and summed in bfloat16 or wider, within the bound.
No kernel may reach another device: no remote copies, remote signals or barrier semaphores. Data moves between devices by JAX's collectives and lax.ppermute only.
A program may use at most 128 MiB of HBM per device.

v0:
```python
import functools

import jax
import jax.numpy as jnp
import numpy as np
from jax import lax
from jax.experimental import pallas as pl
from jax.experimental.pallas import tpu as pltpu
from jax.sharding import PartitionSpec as P

M = 200
RUN = 8
PAD = 256
SLABS = 8
DAMPING = 1.0
VMEM_BYTES = 48 * 1024 * 1024
F32 = jnp.float32
HIGHEST = lax.Precision.HIGHEST
STEADY = pl.CostEstimate(flops=10_000_000_000, bytes_accessed=30_000_000, transcendentals=0)
LITTLE = pl.CostEstimate(flops=1024, bytes_accessed=1024, transcendentals=0)
CUTS = 2
HALVES = 2
FLIGHT = 2
FIRST_SWAPS = ((1, 1), (2, 2))
SWAPS = {2: (4, 2), 3: (6, 2), 5: (8, 4), 8: (12, 2), 9: (14, 2)}
SWAP_WAITS = {5: 6, 10: 12}
RAW_STEP = 2
INVERSE_STEP = 2
FINISHED_AHEAD = 1
ME, PARTNER, NEAR, NEAR_PARTNER, INNER, FIXED = 0, 1, 2, 3, 4, 5
LANES = 128
CODE_ROWS = 16
LEVELS = 32700.0
ROUNDER = 1.5 * 2.0**23
CODES_PER_OCTAVE = 128.0
SMALLEST = 2.0**-110
CHUNK_ORDER = ((2, 3, 1, 0), (0, 2, 3, 1), (3, 1, 0, 2), (1, 0, 2, 3))
SENDS = (
    (((0, 1), (1, 0), (2, 3), (3, 2)),),
    (((0, 1), (3, 2)), ((1, 2), (2, 1))),
    (((0, 1), (1, 3), (2, 0), (3, 2)),),
)


def incidence(earlier, later, rows):
    shape = (rows, earlier.shape[1])
    date = lax.broadcasted_iota(jnp.int32, shape, 0)
    return (date == later).astype(F32) - (date == earlier).astype(F32)


def split_product(left, right):
    def halves(value):
        high = value.astype(jnp.bfloat16)
        return high, (value - high.astype(F32)).astype(jnp.bfloat16)

    left_high, left_low = halves(left)
    right_high, right_low = halves(right)
    small = jnp.dot(left_high, right_low, preferred_element_type=F32) + jnp.dot(left_low, right_high, preferred_element_type=F32)
    return jnp.dot(left_high, right_high, preferred_element_type=F32) + small


def full_product(left, right):
    return jnp.dot(left, right, precision=HIGHEST, preferred_element_type=F32)


def inverse_kernel(counts_ref, pairs_ref, *rest):
    out_ref = rest[-1]
    runs = out_ref.shape[0]
    design = incidence(pairs_ref[0:1, :], pairs_ref[1:2, :], PAD)
    pair = lax.broadcasted_iota(jnp.int32, design.shape, 1)
    contract_last = (((1,), (1,)), ((), ()))
    row = lax.broadcasted_iota(jnp.int32, (PAD, PAD), 0)
    col = lax.broadcasted_iota(jnp.int32, (PAD, PAD), 1)
    identity = (row == col).astype(F32)
    grams = []
    for run in range(runs):
        kept = jnp.where(pair < counts_ref[run], design, 0.0).astype(jnp.bfloat16)
        gram = lax.dot_general(kept, kept, contract_last, preferred_element_type=F32)
        grams.append(gram + DAMPING * identity)
    low = DAMPING
    high = 2.0 * functools.reduce(jnp.maximum, [jnp.max(gram) for gram in grams]) - DAMPING
    total, width = high + low, high - low
    scale = 2.0 * total * total - width * width
    starts = tuple((8.0 * total / scale) * identity - (8.0 / scale) * gram for gram in grams)
    needed = 18.0 * scale / (8.0 * high * low)
    steps = jnp.int32(0)
    for power in range(1, 16):
        steps += (needed > float(2**power)).astype(jnp.int32)

    def newton(product, guesses):
        products = [product(gram, guess) for gram, guess in zip(grams, guesses)]
        return tuple(2.0 * guess - product(guess, each) for guess, each in zip(guesses, products))

    full_steps = 1 + (high > 100.0).astype(jnp.int32)
    guesses = lax.fori_loop(0, steps + 1 - full_steps, lambda _, guesses: newton(split_product, guesses), starts)
    guesses = lax.fori_loop(0, full_steps, lambda _, guesses: newton(full_product, guesses), guesses)
    for run, guess in enumerate(guesses):
        out_ref[run] = guess


def invert_classes(date_pairs, run_counts, after):
    shape = (run_counts.shape[0], PAD, PAD)
    return pl.pallas_call(
        inverse_kernel,
        out_shape=jax.ShapeDtypeStruct(shape, F32),
        grid_spec=pltpu.PrefetchScalarGridSpec(
            num_scalar_prefetch=1,
            grid=(1,),
            in_specs=[pl.BlockSpec(date_pairs.shape, lambda i, c: (0, 0))] + [pl.BlockSpec(memory_space=pl.ANY)] * len(after),
            out_specs=pl.BlockSpec(shape, lambda i, c: (0, 0, 0)),
        ),
        compiler_params=pltpu.CompilerParams(vmem_limit_bytes=VMEM_BYTES),
        cost_estimate=LITTLE,
        name="invert_classes_0",
    )(run_counts, date_pairs, *after)


def sum_solve_kernel(tiles, counts_ref, pairs_ref, data_ref, inverse_ref, out_ref):
    run = pl.program_id(0) // tiles
    design = incidence(pairs_ref[0:1, :], pairs_ref[1:2, :], PAD)
    pair = lax.broadcasted_iota(jnp.int32, design.shape, 1)
    kept = jnp.where(pair < counts_ref[run], design, 0.0).astype(jnp.bfloat16)
    sums = jnp.dot(kept, data_ref[...], preferred_element_type=F32)
    out_ref[...] = jnp.dot(inverse_ref[0, :M, :], sums, precision=HIGHEST, preferred_element_type=F32)


def sum_solve(run_counts, date_pairs, received, inverse):
    runs = run_counts.shape[0]
    total_pairs, pixels = received.shape
    run_pixels = pixels // runs
    tile = run_pixels // 2
    tiles = run_pixels // tile
    return pl.pallas_call(
        functools.partial(sum_solve_kernel, tiles),
        out_shape=jax.ShapeDtypeStruct((M, pixels), F32),
        grid_spec=pltpu.PrefetchScalarGridSpec(
            num_scalar_prefetch=1,
            grid=(runs * tiles,),
            in_specs=[
                pl.BlockSpec(date_pairs.shape, lambda i, c: (0, 0)),
                pl.BlockSpec((total_pairs, tile), lambda i, c: (0, i)),
                pl.BlockSpec((1, PAD, PAD), lambda i, c: (i // tiles, 0, 0)),
            ],
            out_specs=pl.BlockSpec((M, tile), lambda i, c: (0, i)),
        ),
        compiler_params=pltpu.CompilerParams(vmem_limit_bytes=VMEM_BYTES),
        name="sum_solve",
    )(run_counts, date_pairs, received, inverse)


def coded_rows(piece):
    return M * (piece // LANES) + CODE_ROWS


def decode(coded_ref, codes_ref, lots, first):
    coded = coded_ref[...].astype(jnp.int32).astype(F32)
    values = jnp.concatenate([coded[lot * M : (lot + 1) * M, :] for lot in range(lots)], axis=1)
    codes = codes_ref[...].astype(jnp.int32).astype(F32)
    codes = jnp.concatenate([codes[first + lot : first + lot + 1, :] for lot in range(lots)], axis=1)
    return values, jnp.exp2(codes * (1.0 / CODES_PER_OCTAVE)) * (1.0 / LEVELS)


def encode(sums):
    largest = jnp.max(jnp.abs(sums), axis=0, keepdims=True)
    code = jnp.ceil(jnp.log2(jnp.maximum(largest, SMALLEST)) * CODES_PER_OCTAVE)
    scaled = (sums * (LEVELS / jnp.exp2(code * (1.0 / CODES_PER_OCTAVE))) + ROUNDER) - ROUNDER
    lots = sums.shape[1] // LANES
    return jnp.concatenate([scaled[:, lot * LANES : (lot + 1) * LANES] for lot in range(lots)], axis=0), code


def whole(values):
    return values.astype(jnp.int32).astype(jnp.int16)


def piece_count(at, layout, table, counts):
    parts, _, _, shifts = layout
    run = at % parts // CUTS
    return counts[table[shifts + at] * (parts // CUTS) + run]


def pair_sums(count, table, pairs_ref, first_ref, second_ref, members=(ME, PARTNER)):
    width = first_ref.shape[0]
    lane = lax.broadcasted_iota(jnp.int32, (1, 2 * width), 1)
    pair = jnp.where(lane < width, table[members[0]] * width + lane, table[members[1]] * width + lane - width)
    dates = pairs_ref[:, members[0] * width : (members[0] + 2) * width]
    design = incidence(dates[0:1, :], dates[1:2, :], M)
    kept = jnp.where(pair < count, design, 0.0).astype(jnp.bfloat16)
    data = jnp.concatenate([first_ref[...], second_ref[...]], axis=0)
    return jnp.dot(kept, data, preferred_element_type=F32)


def near_sums(wanted, count, table, pairs_ref, raw_refs):
    return pair_sums(jnp.where(wanted, count, 0), table, pairs_ref, *raw_refs, members=(NEAR, NEAR_PARTNER))


def step_kernel(at, layout, adds, swaps, halves, table, counts, pairs_ref, own_ref, partner_ref, *rest):
    if swaps:
        rest[-1][...] = rest[0][...]
        coded_ref, rest = rest[-2], rest[1:]
    else:
        coded_ref = rest[-1]
    count = piece_count(at, layout, table, counts)
    width = own_ref.shape[1] // halves
    lots = width // LANES
    codes = []
    for half in range(halves):
        part = pl.ds(half * width, width)
        sums = pair_sums(count, table, pairs_ref, own_ref.at[:, part], partner_ref.at[:, part])
        if adds == 1:
            rows = pl.ds(half * lots * M, lots * M)
            values, scale = decode(rest[0].at[rows, :], rest[0].at[halves * lots * M :, :], lots, half * lots)
            sums = sums + values * (scale * table[INNER].astype(F32))
        if adds == 2:
            sums = sums + near_sums(table[INNER] == 1, count, table, pairs_ref, [raw_ref.at[:, part] for raw_ref in rest[:2]])
        scaled, code = encode(sums)
        coded_ref[half * lots * M : (half + 1) * lots * M, :] = whole(scaled)
        codes += [code[:, lot * LANES : (lot + 1) * LANES] for lot in range(lots)]
    codes += [jnp.zeros((CODE_ROWS - len(codes), LANES), F32)]
    coded_ref[halves * lots * M :, :] = whole(jnp.concatenate(codes, axis=0))


def step(at, swap, layout, scalars, pairs, phases, partner, earlier, after, piece):
    partner, place_in = partner
    local_pairs = phases.shape[0]
    _, blocks, away, _ = layout
    coded_shape = (coded_rows(piece), LANES)
    in_specs = [
        pl.BlockSpec(pairs.shape, lambda i, t, c: (0, 0)),
        pl.BlockSpec((local_pairs, piece), lambda i, t, c: (0, t[blocks + at])),
        pl.BlockSpec((local_pairs, piece), lambda i, t, c: (0, place_in)),
    ]
    operands = [pairs, phases, partner]
    out_shape = [jax.ShapeDtypeStruct(coded_shape, jnp.int16)]
    out_specs = [pl.BlockSpec(coded_shape, lambda i, t, c: (0, 0))]
    if swap is not None:
        first, count = swap
        wide = piece * count
        in_specs.append(pl.BlockSpec((local_pairs, wide), lambda i, t, c: (0, t[away + first] // count)))
        operands.append(phases)
        out_shape.append(jax.ShapeDtypeStruct((local_pairs, wide), phases.dtype))
        out_specs.append(pl.BlockSpec((local_pairs, wide), lambda i, t, c: (0, 0)))
    in_specs += [pl.BlockSpec(each.shape, lambda i, t, c: (0, 0)) for each in earlier]
    operands += earlier
    in_specs += [pl.BlockSpec(memory_space=pl.ANY)] * len(after)
    results = pl.pallas_call(
        functools.partial(step_kernel, at, layout, len(earlier), swap is not None, HALVES),
        out_shape=out_shape,
        grid_spec=pltpu.PrefetchScalarGridSpec(
            num_scalar_prefetch=2,
            grid=(1,),
            in_specs=in_specs,
            out_specs=out_specs,
        ),
        compiler_params=pltpu.CompilerParams(vmem_limit_bytes=VMEM_BYTES),
        cost_estimate=STEADY,
        name=f"sum_step_{at:02d}",
    )(*scalars, *operands, *after)
    return results[0], results[1] if swap is not None else None


def coded_specs(piece, tiles, index):
    lots = piece // LANES
    return [
        pl.BlockSpec((lots // tiles * M, LANES), lambda *at: (at[index], 0)),
        pl.BlockSpec((CODE_ROWS, LANES), lambda *at: (lots * M // CODE_ROWS, 0)),
    ]


def add_arrived(sums_ref, refs, tiles):
    lots = sums_ref.shape[1] // LANES
    tile = pl.program_id(0)
    for coded_ref, codes_ref in zip(refs[::2], refs[1::2]):
        parts = [decode(coded_ref, codes_ref, lots, at * lots) for at in range(tiles)]
        scale = functools.reduce(lambda chosen, at: jnp.where(tile == at, parts[at][1], chosen), range(1, tiles), parts[0][1])
        sums_ref[...] += parts[0][0] * scale


def finish_kernel(at, layout, tiles, raw, told, table, counts, pairs_ref, own_ref, partner_ref, inverse_ref, *rest):
    first, middle, last = rest[:2], rest[2:4], rest[4:6]
    sums_ref, rest = rest[-1], rest[:-1]
    if told:
        rest[-1][...] = jnp.zeros_like(rest[-1])
        rest = rest[:-1]
    out_ref = rest[-1]
    count = piece_count(at, layout, table, counts)
    sums_ref[...] = pair_sums(count, table, pairs_ref, own_ref, partner_ref)

    @pl.when(table[INNER] == 0)
    def _():
        if raw:
            sums_ref[...] += near_sums(True, count, table, pairs_ref, first)
        else:
            add_arrived(sums_ref, first, tiles)

    @pl.when(table[INNER] == 1)
    def _():
        add_arrived(sums_ref, middle, tiles)

    add_arrived(sums_ref, last, tiles)
    out_ref[...] = split_product(inverse_ref[0, :M, :M], sums_ref[...])


def finish(at, part, layout, scalars, pairs, phases, partner, inverse, raw, arrived, series, told, pixels, piece):
    partner, place_in = partner
    local_pairs = phases.shape[0]
    blocks = layout[1]
    tiles = HALVES
    tile = piece // tiles
    in_specs = [
        pl.BlockSpec(pairs.shape, lambda i, t, c: (0, 0)),
        pl.BlockSpec((local_pairs, tile), lambda i, t, c: (0, t[blocks + at] * tiles + i)),
        pl.BlockSpec((local_pairs, tile), lambda i, t, c: (0, place_in * tiles + i)),
        pl.BlockSpec((1, PAD, PAD), lambda i, t, c: (part // CUTS, 0, 0)),
    ]
    in_specs += [pl.BlockSpec((local_pairs, tile), lambda i, t, c: (0, i))] * len(raw) + coded_specs(piece, tiles, 0) * len(arrived)
    operands = [*scalars, pairs, phases, partner, inverse, *raw] + [each for each in arrived for _ in range(2)]
    aliases = {}
    if series is not None:
        in_specs.append(pl.BlockSpec(memory_space=pl.ANY))
        aliases = {len(operands): 0}
        operands.append(series)
    out_shape = [jax.ShapeDtypeStruct((M, pixels), F32)]
    out_specs = [pl.BlockSpec((M, tile), lambda i, t, c: (0, part * tiles + i))]
    if told:
        out_shape.append(jax.ShapeDtypeStruct((8, LANES), F32))
        out_specs.append(pl.BlockSpec((8, LANES), lambda i, t, c: (0, 0)))
    return pl.pallas_call(
        functools.partial(finish_kernel, at, layout, tiles, len(raw) > 0, told),
        out_shape=out_shape,
        grid_spec=pltpu.PrefetchScalarGridSpec(
            num_scalar_prefetch=2,
            grid=(tiles,),
            in_specs=in_specs,
            out_specs=out_specs,
            scratch_shapes=[pltpu.VMEM((M, tile), F32)],
        ),
        input_output_aliases=aliases,
        compiler_params=pltpu.CompilerParams(vmem_limit_bytes=VMEM_BYTES),
        cost_estimate=LITTLE,
        name=f"finish_{part}",
    )(*operands)


def line_permutation(links):
    return [(2 * source + side, 2 * target + side) for source, target in links for side in range(2)]


def solve_by_sums(phases, date_pairs, counts_of):
    owner_count = lax.axis_size("ifg")
    line = owner_count // 2
    local_pairs, pixels = phases.shape
    owner_pixels = pixels // owner_count
    runs = counts_of().shape[0]
    parts = runs * CUTS
    piece = owner_pixels // parts
    steps = (line - 1) * parts
    me = lax.axis_index("ifg")

    places = np.repeat(np.array(CHUNK_ORDER), parts, axis=1)
    part_of = np.tile(np.arange(parts), line)
    rows = []
    for device in range(owner_count):
        place, side = device // 2, device % 2
        own = (places[place] * 2 + side) * parts + part_of
        away = (places[place] * 2 + 1 - side) * parts + part_of
        known = [place, line - 1 - place, place ^ 1, line - 1 - (place ^ 1)]
        shift = np.array([known.index(chunk) for chunk in places[place]])
        rows.append(np.concatenate([[device, device ^ 1, device ^ 2, device ^ 3, int(0 < place < line - 1)], own, away, shift]))
    row = lax.dynamic_index_in_dim(jnp.asarray(np.stack(rows), jnp.int32), me, 0, keepdims=False)
    head, pieces = FIXED, line * parts
    layout = (parts, head, head + pieces, head + 2 * pieces)

    swap = [(i, i ^ 1) for i in range(owner_count)]
    partner_of = {}

    def swapped(away, first, count):
        here = lax.ppermute(away, "ifg", swap)
        partner_of.update({first + place: (here, place) for place in range(count)})

    place, side = me // 2, me % 2
    chunk = jnp.where(place < line // 2, 2 - 2 * place, 7 - 2 * place)

    def first_away(column, part, count, after):
        block = (chunk * 2 + column) * parts + part
        if after is not None:
            block, _ = lax.optimization_barrier((block, after))
        return lax.dynamic_slice(phases, (0, block * piece), (local_pairs, count * piece))

    near = line_permutation(SENDS[0][0])
    raw_other = lax.ppermute(first_away(1 - side, 0, 1, None), "ifg", near)
    raw_own = lax.ppermute(first_away(side, 0, 1, None), "ifg", near)
    run_counts = counts_of()
    mirrored = lax.ppermute(run_counts, "ifg", line_permutation([(i, line - 1 - i) for i in range(line)]))
    swapped(first_away(1 - side, *FIRST_SWAPS[0], run_counts), *FIRST_SWAPS[0])
    both = jnp.concatenate([run_counts, mirrored])
    counts = jnp.concatenate([both, lax.ppermute(both, "ifg", line_permutation([(i, i ^ 1) for i in range(line)]))])
    swapped(first_away(1 - side, *FIRST_SWAPS[1], counts), *FIRST_SWAPS[1])
    pairs = jnp.concatenate([lax.dynamic_slice(date_pairs, (0, (me ^ at) * local_pairs), (2, local_pairs)) for at in range(4)], axis=1)
    scalars = (row, counts)

    received, coded, series = [[raw_own, raw_other]], None, None

    def finished(part, series, told):
        at = steps + part
        arrived = [received[place * parts + part][-1] for place in range(1 if part == 0 else 0, line - 1)]
        data = (layout, scalars, pairs, phases, partner_of[at], inverse, raw if part == 0 else [], arrived)
        return finish(at, part, *data, series, told, owner_pixels, piece)

    for at in range(1, steps):
        earlier = [] if at < parts else raw if at == parts else [received[at - parts][0]]
        after = [coded] if at > 1 else []
        after += received[at - FLIGHT] if at >= FLIGHT else []
        if at in SWAP_WAITS:
            after.append(partner_of[SWAP_WAITS[at]][0])
        if at == INVERSE_STEP:
            inverse = invert_classes(date_pairs, run_counts, [coded])
            after.append(inverse)
        if at == steps - 1:
            for part in range(FINISHED_AHEAD):
                series, told = finished(part, series, True)
                after.append(told)
        coded, away = step(at, SWAPS.get(at), layout, scalars, pairs, phases, partner_of[at], earlier, after, piece)
        received.append([lax.ppermute(coded, "ifg", line_permutation(links)) for links in SENDS[at // parts]])
        if at in SWAPS:
            swapped(away, *SWAPS[at])
        if at == RAW_STEP:
            raw_other, _ = lax.optimization_barrier((raw_other, coded))
            raw = [raw_own, lax.ppermute(raw_other, "ifg", swap)]

    for part in range(FINISHED_AHEAD, parts):
        series = finished(part, series, False)[0]
    return series


def solve_by_blocks(phases, date_pairs, counts_of):
    owner_count = lax.axis_size("ifg")
    local_pairs, pixels = phases.shape
    owner_pixels = pixels // owner_count
    run_counts = counts_of()
    outgoing = phases.reshape(local_pairs, owner_count, owner_pixels).transpose(1, 0, 2)
    received = lax.all_to_all(outgoing, "ifg", split_axis=0, concat_axis=0, tiled=True)
    inverse = invert_classes(date_pairs, run_counts, [])
    return sum_solve(run_counts, date_pairs, received.reshape(-1, owner_pixels), inverse)


def local(phases, date_pairs, pair_counts, group_ids):
    local_pairs, _, pixels = phases.shape

    def counts_of():
        strip_groups = lax.dynamic_index_in_dim(group_ids, lax.axis_index("grp"), 0, keepdims=False)[::RUN]
        chosen = strip_groups[:, None] == jnp.arange(pair_counts.shape[0], dtype=jnp.int32)
        return jnp.sum(jnp.where(chosen, pair_counts, 0), axis=1)

    line = lax.axis_size("ifg") == 2 * len(CHUNK_ORDER) and group_ids.shape[1] == 2 * RUN
    by_sums = line and 2 * local_pairs > M and local_pairs % LANES == 0 and lax.axis_size("grp") % 2 == 0
    solve = solve_by_sums if by_sums else solve_by_blocks
    return solve(phases.reshape(local_pairs, pixels), date_pairs, counts_of)[None, :, :]


def solution(mesh):
    in_specs = (P("ifg", "grp", None), P(), P(), P(None, "ifg"))
    out_specs = P("grp", None, "ifg")
    return jax.shard_map(local, mesh=mesh, in_specs=in_specs, out_specs=out_specs, check_vma=False)
```

profile of v0, /device:TPU:0, one launch (start us, length us, event | category | flops | bytes accessed | tf_op | source)
XLA Modules:
  0.0 136.8 jit_solution(117710443251339464)
XLA Ops:
  0.8 0.8 fusion.counts_ref
  1.6 5.1 %collective-permute-start = (s32[2]{0:T(128)S(1)}, s32[2]{0:T(128)S(1)}, u32[]{:S(2)}, u32[]{:S(2)}) collective-permute-start(s32[2]{0:T(128)S(1)} %fusion.counts_ref), channel_id=1, source_target_pairs={{0,24},{4,28},{8,16},{12,20},{16,8},{20,12},{24,0},{28,4},{1,25},{... | collective-permute-start | bytes 32 | tf_op jit(solution)/shard_map/ppermute | solution.py:393
  6.7 1.2 dynamic-slice_bitcast_fusion.1
  8.0 1.6 %collective-permute-start.3 = (bf16[128,1024]{1,0:T(8,128)(2,1)S(1)}, bf16[128,1024]{1,0:T(8,128)(2,1)S(1)}, u32[]{:S(2)}, u32[]{:S(2)}) collective-permute-start(bf16[128,1024]{1,0:T(8,128)(2,1)S(1)} %get-tuple-element.36), channel_id=1, source_target_pairs={{0,4},{4,0},{8,12},{12,8},{16,20},{20,16},{24,28},{28,24},{1,5},{5... | collective-permute-start | bytes 786440 | tf_op jit(solution)/shard_map/ppermute | solution.py:377
  9.5 1.9 %collective-permute-start.4 = (bf16[128,1024]{1,0:T(8,128)(2,1)S(1)}, bf16[128,1024]{1,0:T(8,128)(2,1)S(1)}, u32[]{:S(2)}, u32[]{:S(2)}) collective-permute-start(bf16[128,1024]{1,0:T(8,128)(2,1)S(1)} %get-tuple-element.37), channel_id=1, source_target_pairs={{0,8},{4,12},{8,0},{12,4},{16,24},{20,28},{24,16},{28,20},{1,9},{5... | collective-permute-start | bytes 786440 | tf_op jit(solution)/shard_map/ppermute | solution.py:391
  11.5 0.7 fusion.1.table
  12.2 0.7 constant_dynamic-slice_fusion.3
  13.1 8.3 %collective-permute-done.1 = s32[4]{0:T(128)S(1)} collective-permute-done((s32[4]{0:T(128)S(1)}, s32[4]{0:T(128)S(1)}, u32[]{:S(2)}, u32[]{:S(2)}) %collective-permute-start.1) | collective-permute-done | bytes 48 | tf_op jit(solution)/shard_map/ppermute | solution.py:396
  21.5 1.1 dynamic-slice_bitcast_fusion
  22.6 1.6 %collective-permute-start.2 = (bf16[128,2048]{1,0:T(8,128)(2,1)S(1)}, bf16[128,2048]{1,0:T(8,128)(2,1)S(1)}, u32[]{:S(2)}, u32[]{:S(2)}) collective-permute-start(bf16[128,2048]{1,0:T(8,128)(2,1)S(1)} %dynamic-slice_bitcast_fusion), channel_id=1, source_target_pairs={{0,4},{4,0},{8,12},{12,8},{16,20},{20,16},{24,28},{28,24},{1,5},{5... | collective-permute-start | bytes 1572872 | tf_op jit(solution)/shard_map/ppermute | solution.py:377
  24.1 2.0 %sum_step_01.1.rest_0_.rest_1_ = s16[1616,128]{1,0:T(8,128)(2,1)S(1)} custom-call(s32[53]{0:T(128)S(1)} %fusion.1.table, s32[8]{0:T(128)S(1)} %pad_add_fusion.2.counts, s32[2,512]{1,0:T(2,128)S(1)} %pad_add_fusion.pairs_ref, bf16[128,32768]{1,0:T(8,128)(2,1)} %bitcast.14, bf16[128,1024]{1,0:T(8,128)(2,1)S(1)} %collective-permute-done.3.partner_ref), custom_call_target="tpu_custom_call" | custom-call | flops 10000000000 | bytes 30000000 | tf_op jit(solution)/shard_map/sum_step_01/pallas_call | solution.py:245
  26.5 7.6 %invert_classes_0.1.rest_4_.inverse_ref = f32[2,256,256]{2,1,0:T(8,128)S(1)} custom-call(s32[2]{0:T(128)S(1)} %fusion.counts_ref, s32[2,1024]{1,0:T(2,128)S(1)} %copy-done.1, s16[1616,128]{1,0:T(8,128)(2,1)S(1)} %sum_step_01.1.rest_0_.rest_1_), custom_call_target="tpu_custom_call" | custom-call | flops 1024 | bytes 1024 | tf_op jit(solution)/shard_map/invert_classes_0/pallas_call | solution.py:103
  34.0 1.0 collective-permute-done.2.partner_ref
  35.0 2.2 %sum_step_02.1 = (s16[1616,128]{1,0:T(8,128)(2,1)S(1)}, bf16[128,2048]{1,0:T(8,128)(2,1)S(1)}) custom-call(s32[53]{0:T(128)S(1)} %fusion.1.table, s32[8]{0:T(128)S(1)} %pad_add_fusion.2.counts, s32[2,512]{1,0:T(2,128)S(1)} %pad_add_fusion.pairs_ref, bf16[128,32768]{1,0:T(8,128)(2,1)} %bitcast.15, bf16[128,2048]{1,0:T(8,128)(2,1)S(1)} %collective-permute-done.2.partner_ref, ...), custom_call_target="tpu_custom_call" | custom-call | flops 10000000000 | bytes 30000000 | tf_op jit(solution)/shard_map/sum_step_02/pallas_call | solution.py:245
  37.2 0.8 collective-permute-start.9
  38.0 1.3 collective-permute-start.8
  40.1 2.2 %sum_step_03.1 = (s16[1616,128]{1,0:T(8,128)(2,1)S(1)}, bf16[128,2048]{1,0:T(8,128)(2,1)S(1)}) custom-call(s32[53]{0:T(128)S(1)} %fusion.1.table, s32[8]{0:T(128)S(1)} %pad_add_fusion.2.counts, s32[2,512]{1,0:T(2,128)S(1)} %pad_add_fusion.pairs_ref, bf16[128,32768]{1,0:T(8,128)(2,1)} %bitcast.17, bf16[128,2048]{1,0:T(8,128)(2,1)S(1)} %collective-permute-done.2.partner_ref, ...), custom_call_target="tpu_custom_call" | custom-call | flops 10000000000 | bytes 30000000 | tf_op jit(solution)/shard_map/sum_step_03/pallas_call | solution.py:245
  42.3 1.3 collective-permute-start.10
  43.6 1.5 %collective-permute-start.11 = (bf16[128,2048]{1,0:T(8,128)(2,1)S(1)}, bf16[128,2048]{1,0:T(8,128)(2,1)S(1)}, u32[]{:S(2)}, u32[]{:S(2)}) collective-permute-start(bf16[128,2048]{1,0:T(8,128)(2,1)S(1)} %get-tuple-element.26), channel_id=1, source_target_pairs={{0,4},{4,0},{8,12},{12,8},{16,20},{20,16},{24,28},{28,24},{1,5},{5... | collective-permute-start | bytes 1572872 | tf_op jit(solution)/shard_map/ppermute | solution.py:377
  45.1 2.2 %collective-permute-done.8.rest_1_ = bf16[128,1024]{1,0:T(8,128)(2,1)S(1)} collective-permute-done((bf16[128,1024]{1,0:T(8,128)(2,1)S(1)}, bf16[128,1024]{1,0:T(8,128)(2,1)S(1)}, u32[]{:S(2)}, u32[]{:S(2)}) %collective-permute-start.8) | collective-permute-done | bytes 262176 | tf_op jit(solution)/shard_map/ppermute | solution.py:428
  47.3 2.5 %collective-permute-done.9.rest_3_.rest_0_.rest_1_ = s16[1616,128]{1,0:T(8,128)(2,1)S(1)} collective-permute-done((s16[1616,128]{1,0:T(8,128)(2,1)S(1)}, s16[1616,128]{1,0:T(8,128)(2,1)S(1)}, u32[]{:S(2)}, u32[]{:S(2)}) %collective-permute-start.9) | collective-permute-done | bytes 413728 | tf_op jit(solution)/shard_map/ppermute | solution.py:423
  49.8 8.7 %collective-permute-done.6.partner_ref = bf16[128,2048]{1,0:T(8,128)(2,1)S(1)} collective-permute-done((bf16[128,2048]{1,0:T(8,128)(2,1)S(1)}, bf16[128,2048]{1,0:T(8,128)(2,1)S(1)}, u32[]{:S(2)}, u32[]{:S(2)}) %collective-permute-start.6) | collective-permute-done | bytes 524320 | tf_op jit(solution)/shard_map/ppermute | solution.py:377
  58.5 2.0 %sum_step_04.1.rest_2_ = s16[1616,128]{1,0:T(8,128)(2,1)S(1)} custom-call(s32[53]{0:T(128)S(1)} %fusion.1.table, s32[8]{0:T(128)S(1)} %pad_add_fusion.2.counts, s32[2,512]{1,0:T(2,128)S(1)} %pad_add_fusion.pairs_ref, bf16[128,32768]{1,0:T(8,128)(2,1)} %bitcast.19, bf16[128,2048]{1,0:T(8,128)(2,1)S(1)} %collective-permute-done.6.partner_ref, ...), custom_call_target="tpu_custom_call" | custom-call | flops 10000000000 | bytes 30000000 | tf_op jit(solution)/shard_map/sum_step_04/pallas_call | solution.py:245
  61.2 4.4 %collective-permute-start.14 = (s16[1616,128]{1,0:T(8,128)(2,1)S(1)}, s16[1616,128]{1,0:T(8,128)(2,1)S(1)}, u32[]{:S(2)}, u32[]{:S(2)}) collective-permute-start(s16[1616,128]{1,0:T(8,128)(2,1)S(1)} %sum_step_04.1.rest_2_), channel_id=1, source_target_pairs={{0,8},{4,12},{24,16},{28,20},{1,9},{5,13},{25,17},{29,21},{2,10},{... | collective-permute-start | bytes 1241096 | tf_op jit(solution)/shard_map/ppermute | solution.py:423
  65.7 0.8 collective-permute-done.11.rest_4_.partner_ref
  66.5 2.4 %sum_step_05.1 = (s16[1616,128]{1,0:T(8,128)(2,1)S(1)}, bf16[128,4096]{1,0:T(8,128)(2,1)S(1)}) custom-call(s32[53]{0:T(128)S(1)} %fusion.1.table, s32[8]{0:T(128)S(1)} %pad_add_fusion.2.counts, s32[2,512]{1,0:T(2,128)S(1)} %pad_add_fusion.pairs_ref, bf16[128,32768]{1,0:T(8,128)(2,1)} %bitcast.20, bf16[128,2048]{1,0:T(8,128)(2,1)S(1)} %collective-permute-done.6.partner_ref, ...), custom_call_target="tpu_custom_call" | custom-call | flops 10000000000 | bytes 30000000 | tf_op jit(solution)/shard_map/sum_step_05/pallas_call | solution.py:245
  69.6 4.2 %collective-permute-start.13 = (s16[1616,128]{1,0:T(8,128)(2,1)S(1)}, s16[1616,128]{1,0:T(8,128)(2,1)S(1)}, u32[]{:S(2)}, u32[]{:S(2)}) collective-permute-start(s16[1616,128]{1,0:T(8,128)(2,1)S(1)} %get-tuple-element.28.rest_1_), channel_id=1, source_target_pairs={{0,8},{4,12},{24,16},{28,20},{1,9},{5,13},{25,17},{29,21},{2,10},{... | collective-permute-start | bytes 1241096 | tf_op jit(solution)/shard_map/ppermute | solution.py:423
  73.8 1.5 %collective-permute-start.12 = (bf16[128,4096]{1,0:T(8,128)(2,1)S(1)}, bf16[128,4096]{1,0:T(8,128)(2,1)S(1)}, u32[]{:S(2)}, u32[]{:S(2)}) collective-permute-start(bf16[128,4096]{1,0:T(8,128)(2,1)S(1)} %get-tuple-element.27), channel_id=1, source_target_pairs={{0,4},{4,0},{8,12},{12,8},{16,20},{20,16},{24,28},{28,24},{1,5},{5... | collective-permute-start | bytes 3145736 | tf_op jit(solution)/shard_map/ppermute | solution.py:377
  75.2 2.0 %sum_step_06.1.rest_1_ = s16[1616,128]{1,0:T(8,128)(2,1)S(1)} custom-call(s32[53]{0:T(128)S(1)} %fusion.1.table, s32[8]{0:T(128)S(1)} %pad_add_fusion.2.counts, s32[2,512]{1,0:T(2,128)S(1)} %pad_add_fusion.pairs_ref, bf16[128,32768]{1,0:T(8,128)(2,1)} %bitcast.22, bf16[128,2048]{1,0:T(8,128)(2,1)S(1)} %collective-permute-done.11.rest_4_.partner_ref, ...), custom_call_target="tpu_custom_call" | custom-call | flops 10000000000 | bytes 30000000 | tf_op jit(solution)/shard_map/sum_step_06/pallas_call | solution.py:245
  77.9 4.8 %collective-permute-start.17 = (s16[1616,128]{1,0:T(8,128)(2,1)S(1)}, s16[1616,128]{1,0:T(8,128)(2,1)S(1)}, u32[]{:S(2)}, u32[]{:S(2)}) collective-permute-start(s16[1616,128]{1,0:T(8,128)(2,1)S(1)} %sum_step_06.1.rest_1_), channel_id=1, source_target_pairs={{0,8},{4,12},{24,16},{28,20},{1,9},{5,13},{25,17},{29,21},{2,10},{... | collective-permute-start | bytes 1241096 | tf_op jit(solution)/shard_map/ppermute | solution.py:423
  82.7 2.0 %sum_step_07.1.rest_2_ = s16[1616,128]{1,0:T(8,128)(2,1)S(1)} custom-call(s32[53]{0:T(128)S(1)} %fusion.1.table, s32[8]{0:T(128)S(1)} %pad_add_fusion.2.counts, s32[2,512]{1,0:T(2,128)S(1)} %pad_add_fusion.pairs_ref, bf16[128,32768]{1,0:T(8,128)(2,1)} %bitcast.23, bf16[128,2048]{1,0:T(8,128)(2,1)S(1)} %collective-permute-done.11.rest_4_.partner_ref, ...), custom_call_target="tpu_custom_call" | custom-call | flops 10000000000 | bytes 30000000 | tf_op jit(solution)/shard_map/sum_step_07/pallas_call | solution.py:245
  85.4 8.5 %collective-permute-start.19 = (s16[1616,128]{1,0:T(8,128)(2,1)S(1)}, s16[1616,128]{1,0:T(8,128)(2,1)S(1)}, u32[]{:S(2)}, u32[]{:S(2)}) collective-permute-start(s16[1616,128]{1,0:T(8,128)(2,1)S(1)} %sum_step_07.1.rest_2_), channel_id=1, source_target_pairs={{0,8},{4,12},{24,16},{28,20},{1,9},{5,13},{25,17},{29,21},{2,10},{... | collective-permute-start | bytes 1241096 | tf_op jit(solution)/shard_map/ppermute | solution.py:423
  93.9 1.2 collective-permute-done.12.partner_ref
  95.1 2.2 %sum_step_08.1 = (s16[1616,128]{1,0:T(8,128)(2,1)S(1)}, bf16[128,2048]{1,0:T(8,128)(2,1)S(1)}) custom-call(s32[53]{0:T(128)S(1)} %fusion.1.table, s32[8]{0:T(128)S(1)} %pad_add_fusion.2.counts, s32[2,512]{1,0:T(2,128)S(1)} %pad_add_fusion.pairs_ref, bf16[128,32768]{1,0:T(8,128)(2,1)} %bitcast.24, bf16[128,4096]{1,0:T(8,128)(2,1)S(1)} %collective-permute-done.12.partner_ref, ...), custom_call_target="tpu_custom_call" | custom-call | flops 10000000000 | bytes 30000000 | tf_op jit(solution)/shard_map/sum_step_08/pallas_call | solution.py:245
  97.4 1.4 %collective-permute-start.23 = (bf16[128,2048]{1,0:T(8,128)(2,1)S(1)}, bf16[128,2048]{1,0:T(8,128)(2,1)S(1)}, u32[]{:S(2)}, u32[]{:S(2)}) collective-permute-start(bf16[128,2048]{1,0:T(8,128)(2,1)S(1)} %get-tuple-element.32), channel_id=1, source_target_pairs={{0,4},{4,0},{8,12},{12,8},{16,20},{20,16},{24,28},{28,24},{1,5},{5... | collective-permute-start | bytes 1572872 | tf_op jit(solution)/shard_map/ppermute | solution.py:377
  98.8 5.1 %collective-permute-done.19.rest_3_.rest_0_ = s16[1616,128]{1,0:T(8,128)(2,1)S(1)} collective-permute-done((s16[1616,128]{1,0:T(8,128)(2,1)S(1)}, s16[1616,128]{1,0:T(8,128)(2,1)S(1)}, u32[]{:S(2)}, u32[]{:S(2)}) %collective-permute-start.19) | collective-permute-done | bytes 413728 | tf_op jit(solution)/shard_map/ppermute | solution.py:423
  103.9 2.2 %sum_step_09.1 = (s16[1616,128]{1,0:T(8,128)(2,1)S(1)}, bf16[128,2048]{1,0:T(8,128)(2,1)S(1)}) custom-call(s32[53]{0:T(128)S(1)} %fusion.1.table, s32[8]{0:T(128)S(1)} %pad_add_fusion.2.counts, s32[2,512]{1,0:T(2,128)S(1)} %pad_add_fusion.pairs_ref, bf16[128,32768]{1,0:T(8,128)(2,1)} %bitcast.26, bf16[128,4096]{1,0:T(8,128)(2,1)S(1)} %collective-permute-done.12.partner_ref, ...), custom_call_target="tpu_custom_call" | custom-call | flops 10000000000 | bytes 30000000 | tf_op jit(solution)/shard_map/sum_step_09/pallas_call | solution.py:245
  106.1 2.5 %collective-permute-start.24 = (s16[1616,128]{1,0:T(8,128)(2,1)S(1)}, s16[1616,128]{1,0:T(8,128)(2,1)S(1)}, u32[]{:S(2)}, u32[]{:S(2)}) collective-permute-start(s16[1616,128]{1,0:T(8,128)(2,1)S(1)} %get-tuple-element.31.rest_1_), channel_id=1, source_target_pairs={{0,8},{4,12},{8,24},{12,28},{16,0},{20,4},{24,16},{28,20},{1,9},{5... | collective-permute-start | bytes 1241096 | tf_op jit(solution)/shard_map/ppermute | solution.py:423
  108.6 1.6 %collective-permute-start.21 = (bf16[128,2048]{1,0:T(8,128)(2,1)S(1)}, bf16[128,2048]{1,0:T(8,128)(2,1)S(1)}, u32[]{:S(2)}, u32[]{:S(2)}) collective-permute-start(bf16[128,2048]{1,0:T(8,128)(2,1)S(1)} %get-tuple-element.30), channel_id=1, source_target_pairs={{0,4},{4,0},{8,12},{12,8},{16,20},{20,16},{24,28},{28,24},{1,5},{5... | collective-permute-start | bytes 1572872 | tf_op jit(solution)/shard_map/ppermute | solution.py:377
  110.2 2.5 %collective-permute-done.22.rest_2_.rest_4_.rest_5_ = s16[1616,128]{1,0:T(8,128)(2,1)S(1)} collective-permute-done((s16[1616,128]{1,0:T(8,128)(2,1)S(1)}, s16[1616,128]{1,0:T(8,128)(2,1)S(1)}, u32[]{:S(2)}, u32[]{:S(2)}) %collective-permute-start.22) | collective-permute-done | bytes 413728 | tf_op jit(solution)/shard_map/ppermute | solution.py:423
  112.7 2.0 %sum_step_10.1.rest_1_ = s16[1616,128]{1,0:T(8,128)(2,1)S(1)} custom-call(s32[53]{0:T(128)S(1)} %fusion.1.table, s32[8]{0:T(128)S(1)} %pad_add_fusion.2.counts, s32[2,512]{1,0:T(2,128)S(1)} %pad_add_fusion.pairs_ref, bf16[128,32768]{1,0:T(8,128)(2,1)} %bitcast.28, bf16[128,4096]{1,0:T(8,128)(2,1)S(1)} %collective-permute-done.12.partner_ref, ...), custom_call_target="tpu_custom_call" | custom-call | flops 10000000000 | bytes 30000000 | tf_op jit(solution)/shard_map/sum_step_10/pallas_call | solution.py:245
  114.8 2.5 %collective-permute-start.26 = (s16[1616,128]{1,0:T(8,128)(2,1)S(1)}, s16[1616,128]{1,0:T(8,128)(2,1)S(1)}, u32[]{:S(2)}, u32[]{:S(2)}) collective-permute-start(s16[1616,128]{1,0:T(8,128)(2,1)S(1)} %sum_step_10.1.rest_1_), channel_id=1, source_target_pairs={{0,8},{4,12},{8,24},{12,28},{16,0},{20,4},{24,16},{28,20},{1,9},{5... | collective-permute-start | bytes 1241096 | tf_op jit(solution)/shard_map/ppermute | solution.py:423
  117.3 3.9 %finish_0.1 = (f32[200,4096]{1,0:T(8,128)}, f32[8,128]{1,0:T(8,128)S(1)}) custom-call(s32[53]{0:T(128)S(1)} %fusion.1.table, s32[8]{0:T(128)S(1)} %pad_add_fusion.2.counts, s32[2,512]{1,0:T(2,128)S(1)} %pad_add_fusion.pairs_ref, bf16[128,32768]{1,0:T(8,128)(2,1)} %bitcast.29, bf16[128,2048]{1,0:T(8,128)(2,1)S(1)} %collective-permute-done.23.rest_3_.partner_ref, ...), custom_call_target="tpu_custom_call" | custom-call | flops 1024 | bytes 1024 | tf_op jit(solution)/shard_map/finish_0/pallas_call | solution.py:327
  121.6 2.0 %sum_step_11.1 = s16[1616,128]{1,0:T(8,128)(2,1)S(1)} custom-call(s32[53]{0:T(128)S(1)} %fusion.1.table, s32[8]{0:T(128)S(1)} %pad_add_fusion.2.counts, s32[2,512]{1,0:T(2,128)S(1)} %pad_add_fusion.pairs_ref, bf16[128,32768]{1,0:T(8,128)(2,1)} %bitcast.30, bf16[128,4096]{1,0:T(8,128)(2,1)S(1)} %collective-permute-done.12.partner_ref, ...), custom_call_target="tpu_custom_call" | custom-call | flops 10000000000 | bytes 30000000 | tf_op jit(solution)/shard_map/sum_step_11/pallas_call | solution.py:245
  123.6 2.5 %collective-permute-start.25 = (s16[1616,128]{1,0:T(8,128)(2,1)S(1)}, s16[1616,128]{1,0:T(8,128)(2,1)S(1)}, u32[]{:S(2)}, u32[]{:S(2)}) collective-permute-start(s16[1616,128]{1,0:T(8,128)(2,1)S(1)} %sum_step_11.1), channel_id=1, source_target_pairs={{0,8},{4,12},{8,24},{12,28},{16,0},{20,4},{24,16},{28,20},{1,9},{5... | collective-permute-start | bytes 1241096 | tf_op jit(solution)/shard_map/ppermute | solution.py:423
  126.1 3.6 %finish_1.1.rest_6_ = f32[200,4096]{1,0:T(8,128)} custom-call(s32[53]{0:T(128)S(1)} %fusion.1.table, s32[8]{0:T(128)S(1)} %pad_add_fusion.2.counts, s32[2,512]{1,0:T(2,128)S(1)} %pad_add_fusion.pairs_ref, bf16[128,32768]{1,0:T(8,128)(2,1)} %bitcast.31, ...), custom_call_target="tpu_custom_call", output_to_operand_aliasing={{}: (12, {})} | custom-call | flops 1024 | bytes 1024 | tf_op jit(solution)/shard_map/finish_1/pallas_call | solution.py:327
  129.7 3.6 %finish_2.1.rest_6_ = f32[200,4096]{1,0:T(8,128)} custom-call(s32[53]{0:T(128)S(1)} %fusion.1.table, s32[8]{0:T(128)S(1)} %pad_add_fusion.2.counts, s32[2,512]{1,0:T(2,128)S(1)} %pad_add_fusion.pairs_ref, bf16[128,32768]{1,0:T(8,128)(2,1)} %bitcast.32, bf16[128,2048]{1,0:T(8,128)(2,1)S(1)} %collective-permute-done.21.partner_ref, ...), custom_call_target="tpu_custom_call", output_to_operand_aliasing={{}: (12, {})} | custom-call | flops 1024 | bytes 1024 | tf_op jit(solution)/shard_map/finish_2/pallas_call | solution.py:327
  133.3 3.6 %finish_3.1 = f32[200,4096]{1,0:T(8,128)} custom-call(s32[53]{0:T(128)S(1)} %fusion.1.table, s32[8]{0:T(128)S(1)} %pad_add_fusion.2.counts, s32[2,512]{1,0:T(2,128)S(1)} %pad_add_fusion.pairs_ref, bf16[128,32768]{1,0:T(8,128)(2,1)} %bitcast.33, bf16[128,2048]{1,0:T(8,128)(2,1)S(1)} %collective-permute-done.21.partner_ref, ...), custom_call_target="tpu_custom_call", output_to_operand_aliasing={{}: (12, {})} | custom-call | flops 1024 | bytes 1024 | tf_op jit(solution)/shard_map/finish_3/pallas_call | solution.py:327
  (36 shorter events, 5.4 us)
Async XLA Ops:
  0.0 0.7 copy-start
  1.6 11.3 %collective-permute-start = (s32[2]{0:T(128)S(1)}, s32[2]{0:T(128)S(1)}, u32[]{:S(2)}, u32[]{:S(2)}) collective-permute-start(s32[2]{0:T(128)S(1)} %fusion.counts_ref), channel_id=1, source_target_pairs={{0,24},{4,28},{8,16},{12,20},{16,8},{20,12},{24,0},{28,4},{1,25},{... | collective-permute-start | bytes 32 | tf_op jit(solution)/shard_map/ppermute | solution.py:393
  7.9 26.1 %collective-permute-start.5 = (bf16[128,1024]{1,0:T(8,128)(2,1)S(1)}, bf16[128,1024]{1,0:T(8,128)(2,1)S(1)}, u32[]{:S(2)}, u32[]{:S(2)}) collective-permute-start(bf16[128,1024]{1,0:T(8,128)(2,1)S(1)} %get-tuple-element.35), channel_id=1, source_target_pairs={{0,8},{4,12},{8,0},{12,4},{16,24},{20,28},{24,16},{28,20},{1,9},{5... | collective-permute-start | bytes 786440 | tf_op jit(solution)/shard_map/ppermute | solution.py:390
  8.0 16.2 %collective-permute-start.3 = (bf16[128,1024]{1,0:T(8,128)(2,1)S(1)}, bf16[128,1024]{1,0:T(8,128)(2,1)S(1)}, u32[]{:S(2)}, u32[]{:S(2)}) collective-permute-start(bf16[128,1024]{1,0:T(8,128)(2,1)S(1)} %get-tuple-element.36), channel_id=1, source_target_pairs={{0,4},{4,0},{8,12},{12,8},{16,20},{20,16},{24,28},{28,24},{1,5},{5... | collective-permute-start | bytes 786440 | tf_op jit(solution)/shard_map/ppermute | solution.py:377
  9.5 24.5 %collective-permute-start.4 = (bf16[128,1024]{1,0:T(8,128)(2,1)S(1)}, bf16[128,1024]{1,0:T(8,128)(2,1)S(1)}, u32[]{:S(2)}, u32[]{:S(2)}) collective-permute-start(bf16[128,1024]{1,0:T(8,128)(2,1)S(1)} %get-tuple-element.37), channel_id=1, source_target_pairs={{0,8},{4,12},{8,0},{12,4},{16,24},{20,28},{24,16},{28,20},{1,9},{5... | collective-permute-start | bytes 786440 | tf_op jit(solution)/shard_map/ppermute | solution.py:391
  13.0 8.4 %collective-permute-start.1 = (s32[4]{0:T(128)S(1)}, s32[4]{0:T(128)S(1)}, u32[]{:S(2)}, u32[]{:S(2)}) collective-permute-start(s32[4]{0:T(128)S(1)} %pad_add_fusion.1), channel_id=1, source_target_pairs={{0,8},{4,12},{8,0},{12,4},{16,24},{20,28},{24,16},{28,20},{1,9},{5... | collective-permute-start | bytes 56 | tf_op jit(solution)/shard_map/ppermute | solution.py:396
  22.6 12.5 %collective-permute-start.2 = (bf16[128,2048]{1,0:T(8,128)(2,1)S(1)}, bf16[128,2048]{1,0:T(8,128)(2,1)S(1)}, u32[]{:S(2)}, u32[]{:S(2)}) collective-permute-start(bf16[128,2048]{1,0:T(8,128)(2,1)S(1)} %dynamic-slice_bitcast_fusion), channel_id=1, source_target_pairs={{0,4},{4,0},{8,12},{12,8},{16,20},{20,16},{24,28},{28,24},{1,5},{5... | collective-permute-start | bytes 1572872 | tf_op jit(solution)/shard_map/ppermute | solution.py:377
  24.1 2.3 %copy-start.1 = (s32[2,1024]{1,0:T(2,128)S(1)}, s32[2,1024]{1,0:T(2,128)}, u32[]{:S(2)}) copy-start(s32[2,1024]{1,0:T(2,128)} %pairs_ref.1) | copy-start | bytes 24580
  26.1 14.0 %collective-permute-start.7 = (s16[1616,128]{1,0:T(8,128)(2,1)S(1)}, s16[1616,128]{1,0:T(8,128)(2,1)S(1)}, u32[]{:S(2)}, u32[]{:S(2)}) collective-permute-start(s16[1616,128]{1,0:T(8,128)(2,1)S(1)} %sum_step_01.1.rest_0_.rest_1_), channel_id=1, source_target_pairs={{0,8},{4,12},{8,0},{12,4},{16,24},{20,28},{24,16},{28,20},{1,9},{5... | collective-permute-start | bytes 1241096 | tf_op jit(solution)/shard_map/ppermute | solution.py:423
  37.2 12.6 %collective-permute-start.9 = (s16[1616,128]{1,0:T(8,128)(2,1)S(1)}, s16[1616,128]{1,0:T(8,128)(2,1)S(1)}, u32[]{:S(2)}, u32[]{:S(2)}) collective-permute-start(s16[1616,128]{1,0:T(8,128)(2,1)S(1)} %get-tuple-element.23.rest_1_), channel_id=1, source_target_pairs={{0,8},{4,12},{8,0},{12,4},{16,24},{20,28},{24,16},{28,20},{1,9},{5... | collective-permute-start | bytes 1241096 | tf_op jit(solution)/shard_map/ppermute | solution.py:423
  38.0 9.2 %collective-permute-start.8 = (bf16[128,1024]{1,0:T(8,128)(2,1)S(1)}, bf16[128,1024]{1,0:T(8,128)(2,1)S(1)}, u32[]{:S(2)}, u32[]{:S(2)}) collective-permute-start(bf16[128,1024]{1,0:T(8,128)(2,1)S(1)} %collective-permute-done.5.rest_3_), channel_id=1, source_target_pairs={{0,4},{4,0},{8,12},{12,8},{16,20},{20,16},{24,28},{28,24},{1,5},{5... | collective-permute-start | bytes 786440 | tf_op jit(solution)/shard_map/ppermute | solution.py:428
  39.4 19.1 %collective-permute-start.6 = (bf16[128,2048]{1,0:T(8,128)(2,1)S(1)}, bf16[128,2048]{1,0:T(8,128)(2,1)S(1)}, u32[]{:S(2)}, u32[]{:S(2)}) collective-permute-start(bf16[128,2048]{1,0:T(8,128)(2,1)S(1)} %get-tuple-element.22), channel_id=1, source_target_pairs={{0,4},{4,0},{8,12},{12,8},{16,20},{20,16},{24,28},{28,24},{1,5},{5... | collective-permute-start | bytes 1572872 | tf_op jit(solution)/shard_map/ppermute | solution.py:377
  42.3 23.4 %collective-permute-start.10 = (s16[1616,128]{1,0:T(8,128)(2,1)S(1)}, s16[1616,128]{1,0:T(8,128)(2,1)S(1)}, u32[]{:S(2)}, u32[]{:S(2)}) collective-permute-start(s16[1616,128]{1,0:T(8,128)(2,1)S(1)} %get-tuple-element.25.rest_2_), channel_id=1, source_target_pairs={{0,8},{4,12},{8,0},{12,4},{16,24},{20,28},{24,16},{28,20},{1,9},{5... | collective-permute-start | bytes 1241096 | tf_op jit(solution)/shard_map/ppermute | solution.py:423
  43.6 22.9 %collective-permute-start.11 = (bf16[128,2048]{1,0:T(8,128)(2,1)S(1)}, bf16[128,2048]{1,0:T(8,128)(2,1)S(1)}, u32[]{:S(2)}, u32[]{:S(2)}) collective-permute-start(bf16[128,2048]{1,0:T(8,128)(2,1)S(1)} %get-tuple-element.26), channel_id=1, source_target_pairs={{0,4},{4,0},{8,12},{12,8},{16,20},{20,16},{24,28},{28,24},{1,5},{5... | collective-permute-start | bytes 1572872 | tf_op jit(solution)/shard_map/ppermute | solution.py:377
  60.5 14.7 %collective-permute-start.15 = (s16[1616,128]{1,0:T(8,128)(2,1)S(1)}, s16[1616,128]{1,0:T(8,128)(2,1)S(1)}, u32[]{:S(2)}, u32[]{:S(2)}) collective-permute-start(s16[1616,128]{1,0:T(8,128)(2,1)S(1)} %sum_step_04.1.rest_2_), channel_id=1, source_target_pairs={{8,16},{12,20},{16,8},{20,12},{9,17},{13,21},{17,9},{21,13},{10,18... | collective-permute-start | bytes 1241096 | tf_op jit(solution)/shard_map/ppermute | solution.py:423
  61.2 14.0 %collective-permute-start.14 = (s16[1616,128]{1,0:T(8,128)(2,1)S(1)}, s16[1616,128]{1,0:T(8,128)(2,1)S(1)}, u32[]{:S(2)}, u32[]{:S(2)}) collective-permute-start(s16[1616,128]{1,0:T(8,128)(2,1)S(1)} %sum_step_04.1.rest_2_), channel_id=1, source_target_pairs={{0,8},{4,12},{24,16},{28,20},{1,9},{5,13},{25,17},{29,21},{2,10},{... | collective-permute-start | bytes 1241096 | tf_op jit(solution)/shard_map/ppermute | solution.py:423
  68.9 13.8 %collective-permute-start.16 = (s16[1616,128]{1,0:T(8,128)(2,1)S(1)}, s16[1616,128]{1,0:T(8,128)(2,1)S(1)}, u32[]{:S(2)}, u32[]{:S(2)}) collective-permute-start(s16[1616,128]{1,0:T(8,128)(2,1)S(1)} %get-tuple-element.28.rest_1_), channel_id=1, source_target_pairs={{8,16},{12,20},{16,8},{20,12},{9,17},{13,21},{17,9},{21,13},{10,18... | collective-permute-start | bytes 1241096 | tf_op jit(solution)/shard_map/ppermute | solution.py:423
  69.6 13.1 %collective-permute-start.13 = (s16[1616,128]{1,0:T(8,128)(2,1)S(1)}, s16[1616,128]{1,0:T(8,128)(2,1)S(1)}, u32[]{:S(2)}, u32[]{:S(2)}) collective-permute-start(s16[1616,128]{1,0:T(8,128)(2,1)S(1)} %get-tuple-element.28.rest_1_), channel_id=1, source_target_pairs={{0,8},{4,12},{24,16},{28,20},{1,9},{5,13},{25,17},{29,21},{2,10},{... | collective-permute-start | bytes 1241096 | tf_op jit(solution)/shard_map/ppermute | solution.py:423
  73.8 21.3 %collective-permute-start.12 = (bf16[128,4096]{1,0:T(8,128)(2,1)S(1)}, bf16[128,4096]{1,0:T(8,128)(2,1)S(1)}, u32[]{:S(2)}, u32[]{:S(2)}) collective-permute-start(bf16[128,4096]{1,0:T(8,128)(2,1)S(1)} %get-tuple-element.27), channel_id=1, source_target_pairs={{0,4},{4,0},{8,12},{12,8},{16,20},{20,16},{24,28},{28,24},{1,5},{5... | collective-permute-start | bytes 3145736 | tf_op jit(solution)/shard_map/ppermute | solution.py:377
  77.2 16.7 %collective-permute-start.18 = (s16[1616,128]{1,0:T(8,128)(2,1)S(1)}, s16[1616,128]{1,0:T(8,128)(2,1)S(1)}, u32[]{:S(2)}, u32[]{:S(2)}) collective-permute-start(s16[1616,128]{1,0:T(8,128)(2,1)S(1)} %sum_step_06.1.rest_1_), channel_id=1, source_target_pairs={{8,16},{12,20},{16,8},{20,12},{9,17},{13,21},{17,9},{21,13},{10,18... | collective-permute-start | bytes 1241096 | tf_op jit(solution)/shard_map/ppermute | solution.py:423
  77.9 16.0 %collective-permute-start.17 = (s16[1616,128]{1,0:T(8,128)(2,1)S(1)}, s16[1616,128]{1,0:T(8,128)(2,1)S(1)}, u32[]{:S(2)}, u32[]{:S(2)}) collective-permute-start(s16[1616,128]{1,0:T(8,128)(2,1)S(1)} %sum_step_06.1.rest_1_), channel_id=1, source_target_pairs={{0,8},{4,12},{24,16},{28,20},{1,9},{5,13},{25,17},{29,21},{2,10},{... | collective-permute-start | bytes 1241096 | tf_op jit(solution)/shard_map/ppermute | solution.py:423
  84.7 14.1 %collective-permute-start.20 = (s16[1616,128]{1,0:T(8,128)(2,1)S(1)}, s16[1616,128]{1,0:T(8,128)(2,1)S(1)}, u32[]{:S(2)}, u32[]{:S(2)}) collective-permute-start(s16[1616,128]{1,0:T(8,128)(2,1)S(1)} %sum_step_07.1.rest_2_), channel_id=1, source_target_pairs={{8,16},{12,20},{16,8},{20,12},{9,17},{13,21},{17,9},{21,13},{10,18... | collective-permute-start | bytes 1241096 | tf_op jit(solution)/shard_map/ppermute | solution.py:423
  85.4 18.5 %collective-permute-start.19 = (s16[1616,128]{1,0:T(8,128)(2,1)S(1)}, s16[1616,128]{1,0:T(8,128)(2,1)S(1)}, u32[]{:S(2)}, u32[]{:S(2)}) collective-permute-start(s16[1616,128]{1,0:T(8,128)(2,1)S(1)} %sum_step_07.1.rest_2_), channel_id=1, source_target_pairs={{0,8},{4,12},{24,16},{28,20},{1,9},{5,13},{25,17},{29,21},{2,10},{... | collective-permute-start | bytes 1241096 | tf_op jit(solution)/shard_map/ppermute | solution.py:423
  97.3 15.4 %collective-permute-start.22 = (s16[1616,128]{1,0:T(8,128)(2,1)S(1)}, s16[1616,128]{1,0:T(8,128)(2,1)S(1)}, u32[]{:S(2)}, u32[]{:S(2)}) collective-permute-start(s16[1616,128]{1,0:T(8,128)(2,1)S(1)} %get-tuple-element.29.rest_2_), channel_id=1, source_target_pairs={{0,8},{4,12},{8,24},{12,28},{16,0},{20,4},{24,16},{28,20},{1,9},{5... | collective-permute-start | bytes 1241096 | tf_op jit(solution)/shard_map/ppermute | solution.py:423
  97.4 15.3 %collective-permute-start.23 = (bf16[128,2048]{1,0:T(8,128)(2,1)S(1)}, bf16[128,2048]{1,0:T(8,128)(2,1)S(1)}, u32[]{:S(2)}, u32[]{:S(2)}) collective-permute-start(bf16[128,2048]{1,0:T(8,128)(2,1)S(1)} %get-tuple-element.32), channel_id=1, source_target_pairs={{0,4},{4,0},{8,12},{12,8},{16,20},{20,16},{24,28},{28,24},{1,5},{5... | collective-permute-start | bytes 1572872 | tf_op jit(solution)/shard_map/ppermute | solution.py:377
  106.1 15.5 %collective-permute-start.24 = (s16[1616,128]{1,0:T(8,128)(2,1)S(1)}, s16[1616,128]{1,0:T(8,128)(2,1)S(1)}, u32[]{:S(2)}, u32[]{:S(2)}) collective-permute-start(s16[1616,128]{1,0:T(8,128)(2,1)S(1)} %get-tuple-element.31.rest_1_), channel_id=1, source_target_pairs={{0,8},{4,12},{8,24},{12,28},{16,0},{20,4},{24,16},{28,20},{1,9},{5... | collective-permute-start | bytes 1241096 | tf_op jit(solution)/shard_map/ppermute | solution.py:423
  108.6 21.1 %collective-permute-start.21 = (bf16[128,2048]{1,0:T(8,128)(2,1)S(1)}, bf16[128,2048]{1,0:T(8,128)(2,1)S(1)}, u32[]{:S(2)}, u32[]{:S(2)}) collective-permute-start(bf16[128,2048]{1,0:T(8,128)(2,1)S(1)} %get-tuple-element.30), channel_id=1, source_target_pairs={{0,4},{4,0},{8,12},{12,8},{16,20},{20,16},{24,28},{28,24},{1,5},{5... | collective-permute-start | bytes 1572872 | tf_op jit(solution)/shard_map/ppermute | solution.py:377
  114.8 15.0 %collective-permute-start.26 = (s16[1616,128]{1,0:T(8,128)(2,1)S(1)}, s16[1616,128]{1,0:T(8,128)(2,1)S(1)}, u32[]{:S(2)}, u32[]{:S(2)}) collective-permute-start(s16[1616,128]{1,0:T(8,128)(2,1)S(1)} %sum_step_10.1.rest_1_), channel_id=1, source_target_pairs={{0,8},{4,12},{8,24},{12,28},{16,0},{20,4},{24,16},{28,20},{1,9},{5... | collective-permute-start | bytes 1241096 | tf_op jit(solution)/shard_map/ppermute | solution.py:423
  123.6 9.7 %collective-permute-start.25 = (s16[1616,128]{1,0:T(8,128)(2,1)S(1)}, s16[1616,128]{1,0:T(8,128)(2,1)S(1)}, u32[]{:S(2)}, u32[]{:S(2)}) collective-permute-start(s16[1616,128]{1,0:T(8,128)(2,1)S(1)} %sum_step_11.1), channel_id=1, source_target_pairs={{0,8},{4,12},{8,24},{12,28},{16,0},{20,4},{24,16},{28,20},{1,9},{5... | collective-permute-start | bytes 1241096 | tf_op jit(solution)/shard_map/ppermute | solution.py:423
where the time goes:
time: 138 us; the launch traced here: 137 us
  starting transfers between devices  53 us (38%)
  Pallas kernels  45.3 us (33%)
  waiting for transfers between devices  32.8 us (24%)
  local copies, waits for them, and re-layouts  4.45 us (3%)
    ppermute x15, starting transfers between devices, solve_by_sums(): lax.ppermute(coded, 'ifg', line_permutation(links))  34.8 us
    pallas_call x11, Pallas kernels, step(): pl.pallas_call(functools.partial(step_kernel, at, layout, len(earlier), s...  23.1 us
    pallas_call x4, Pallas kernels, finish(): pl.pallas_call(functools.partial(finish_kernel, at, layout, tiles, len(ra...  14.6 us
    ppermute x7, waiting for transfers between devices, swapped(): here = lax.ppermute(away, 'ifg', swap)  11.7 us
    ppermute x15, waiting for transfers between devices, solve_by_sums(): lax.ppermute(coded, 'ifg', line_permutation(links))  10.6 us
    ppermute x7, starting transfers between devices, swapped(): here = lax.ppermute(away, 'ifg', swap)  9.72 us
    ppermute x1, waiting for transfers between devices, solve_by_sums(): lax.ppermute(both, 'ifg', line_permutation([(i, i ^ 1) for i in range(lin...  8.34 us
    pallas_call x1, Pallas kernels, invert_classes(): pl.pallas_call(inverse_kernel, out_shape=jax.ShapeDtypeStruct(shape, F32)...  7.56 us
  transfers between devices with their start and end apart: 27, of which 10 were waited for; matrix products, arithmetic and copies ran while one was open for 3% of the time, Pallas kernels for 30%

commit v1 on v0

--- a/solution.py
+++ b/solution.py
@@ -363,8 +363,7 @@
         place, side = device // 2, device % 2
         own = (places[place] * 2 + side) * parts + part_of
         away = (places[place] * 2 + 1 - side) * parts + part_of
-        known = [place, line - 1 - place, place ^ 1, line - 1 - (place ^ 1)]
-        shift = np.array([known.index(chunk) for chunk in places[place]])
+        shift = (place - places[place]) % line
         rows.append(np.concatenate([[device, device ^ 1, device ^ 2, device ^ 3, int(0 < place < line - 1)], own, away, shift]))
     row = lax.dynamic_index_in_dim(jnp.asarray(np.stack(rows), jnp.int32), me, 0, keepdims=False)
     head, pieces = FIXED, line * parts
@@ -386,14 +385,16 @@
             block, _ = lax.optimization_barrier((block, after))
         return lax.dynamic_slice(phases, (0, block * piece), (local_pairs, count * piece))
 
+    run_counts = counts_of()
+    counts = [run_counts]
+    for distance in range(1, line):
+        links = [(i, (i + distance) % line) for i in range(line)]
+        counts.append(lax.ppermute(run_counts, "ifg", line_permutation(links)))
+    counts = jnp.concatenate(counts)
+    swapped(first_away(1 - side, *FIRST_SWAPS[0], run_counts), *FIRST_SWAPS[0])
     near = line_permutation(SENDS[0][0])
-    raw_other = lax.ppermute(first_away(1 - side, 0, 1, None), "ifg", near)
-    raw_own = lax.ppermute(first_away(side, 0, 1, None), "ifg", near)
-    run_counts = counts_of()
-    mirrored = lax.ppermute(run_counts, "ifg", line_permutation([(i, line - 1 - i) for i in range(line)]))
-    swapped(first_away(1 - side, *FIRST_SWAPS[0], run_counts), *FIRST_SWAPS[0])
-    both = jnp.concatenate([run_counts, mirrored])
-    counts = jnp.concatenate([both, lax.ppermute(both, "ifg", line_permutation([(i, i ^ 1) for i in range(line)]))])
+    raw_other = lax.ppermute(first_away(1 - side, 0, 1, run_counts), "ifg", near)
+    raw_own = lax.ppermute(first_away(side, 0, 1, run_counts), "ifg", near)
     swapped(first_away(1 - side, *FIRST_SWAPS[1], counts), *FIRST_SWAPS[1])
     pairs = jnp.concatenate([lax.dynamic_slice(date_pairs, (0, (me ^ at) * local_pairs), (2, local_pairs)) for at in range(4)], axis=1)
     scalars = (row, counts)

time: 138 us -> 134 us (0.971)
  starting transfers between devices: 53 us -> 51.1 us
  waiting for transfers between devices: 32.8 us -> 30.9 us
    ppermute x4 -> x5, waiting for transfers between devices: 8.35 us -> 0.01 us  [the longest x3 0.01 us: solve_by_sums(): counts.append(lax.ppermute(run_counts, 'ifg', line_permutation(links)))]
    ppermute x7, waiting for transfers between devices: 11.7 us -> 16.9 us  [swapped(): here = lax.ppermute(away, 'ifg', swap)]
    ppermute x15, starting transfers between devices: 34.8 us -> 31.5 us  [solve_by_sums(): lax.ppermute(coded, 'ifg', line_permutation(links))]
    ppermute x4 -> x5, starting transfers between devices: 7.21 us -> 8.79 us  [the longest x3 6.11 us: solve_by_sums(): counts.append(lax.ppermute(run_counts, 'ifg', line_permutation(links)))]
  transfers between devices with their start and end apart: 27 -> 28, of which waited for: 10 -> 12; matrix products, arithmetic and copies ran while one was open for 3% -> 3% of each run, Pallas kernels for 30% -> 31%
where the time goes in v1:
time: 134 us; the launch traced here: 133 us
  starting transfers between devices  51.1 us (38%)
  Pallas kernels  45.3 us (34%)
  waiting for transfers between devices  30.9 us (23%)
  local copies, waits for them, and re-layouts  4.45 us (3%)
    ppermute x15, starting transfers between devices, solve_by_sums(): lax.ppermute(coded, 'ifg', line_permutation(links))  31.5 us
    pallas_call x11, Pallas kernels, step(): pl.pallas_call(functools.partial(step_kernel, at, layout, len(earlier), s...  23.1 us
    ppermute x7, waiting for transfers between devices, swapped(): here = lax.ppermute(away, 'ifg', swap)  16.9 us
    pallas_call x4, Pallas kernels, finish(): pl.pallas_call(functools.partial(finish_kernel, at, layout, tiles, len(ra...  14.6 us
    ppermute x15, waiting for transfers between devices, solve_by_sums(): lax.ppermute(coded, 'ifg', line_permutation(links))  11.1 us
    ppermute x7, starting transfers between devices, swapped(): here = lax.ppermute(away, 'ifg', swap)  8.51 us
    pallas_call x1, Pallas kernels, invert_classes(): pl.pallas_call(inverse_kernel, out_shape=jax.ShapeDtypeStruct(shape, F32)...  7.56 us
    ppermute x3, starting transfers between devices, solve_by_sums(): counts.append(lax.ppermute(run_counts, 'ifg', line_permutation(links)))  6.11 us
  transfers between devices with their start and end apart: 28, of which 12 were waited for; matrix products, arithmetic and copies ran while one was open for 3% of the time, Pallas kernels for 31%

profile of v1, /device:TPU:0, one launch (start us, length us, event | category | flops | bytes accessed | tf_op | source)
XLA Modules:
  0.0 133.0 jit_solution(4331074980557616873)
XLA Ops:
  0.8 0.8 fusion.counts_ref
  1.6 5.1 %collective-permute-start.2 = (s32[2]{0:T(128)S(1)}, s32[2]{0:T(128)S(1)}, u32[]{:S(2)}, u32[]{:S(2)}) collective-permute-start(s32[2]{0:T(128)S(1)} %fusion.counts_ref), channel_id=1, source_target_pairs={{0,24},{4,28},{8,0},{12,4},{16,8},{20,12},{24,16},{28,20},{1,25},{... | collective-permute-start | bytes 32 | tf_op jit(solution)/shard_map/ppermute | solution.py:392
  6.7 1.0 collective-permute-start
  7.7 1.2 dynamic-slice_bitcast_fusion.1
  8.9 2.5 %collective-permute-start.6 = (bf16[128,1024]{1,0:T(8,128)(2,1)S(1)}, bf16[128,1024]{1,0:T(8,128)(2,1)S(1)}, u32[]{:S(2)}, u32[]{:S(2)}) collective-permute-start(bf16[128,1024]{1,0:T(8,128)(2,1)S(1)} %get-tuple-element.39), channel_id=1, source_target_pairs={{0,8},{4,12},{8,0},{12,4},{16,24},{20,28},{24,16},{28,20},{1,9},{5... | collective-permute-start | bytes 786440 | tf_op jit(solution)/shard_map/ppermute | solution.py:396
  11.4 1.5 %collective-permute-start.4 = (bf16[128,1024]{1,0:T(8,128)(2,1)S(1)}, bf16[128,1024]{1,0:T(8,128)(2,1)S(1)}, u32[]{:S(2)}, u32[]{:S(2)}) collective-permute-start(bf16[128,1024]{1,0:T(8,128)(2,1)S(1)} %get-tuple-element.40), channel_id=1, source_target_pairs={{0,4},{4,0},{8,12},{12,8},{16,20},{20,16},{24,28},{28,24},{1,5},{5... | collective-permute-start | bytes 786440 | tf_op jit(solution)/shard_map/ppermute | solution.py:376
  12.9 0.7 fusion.1.table
  13.6 0.7 constant_dynamic-slice_fusion.3
  14.6 1.1 dynamic-slice_bitcast_fusion
  16.3 3.6 %collective-permute-done.4.partner_ref = bf16[128,1024]{1,0:T(8,128)(2,1)S(1)} collective-permute-done((bf16[128,1024]{1,0:T(8,128)(2,1)S(1)}, bf16[128,1024]{1,0:T(8,128)(2,1)S(1)}, u32[]{:S(2)}, u32[]{:S(2)}) %collective-permute-start.4) | collective-permute-done | bytes 262176 | tf_op jit(solution)/shard_map/ppermute | solution.py:376
  19.9 2.0 %sum_step_01.1.rest_0_.rest_1_ = s16[1616,128]{1,0:T(8,128)(2,1)S(1)} custom-call(s32[53]{0:T(128)S(1)} %fusion.1.table, s32[8]{0:T(128)S(1)} %pad_add_fusion.1.counts, s32[2,512]{1,0:T(2,128)S(1)} %pad_add_fusion.pairs_ref, bf16[128,32768]{1,0:T(8,128)(2,1)} %bitcast.14, bf16[128,1024]{1,0:T(8,128)(2,1)S(1)} %collective-permute-done.4.partner_ref), custom_call_target="tpu_custom_call" | custom-call | flops 10000000000 | bytes 30000000 | tf_op jit(solution)/shard_map/sum_step_01/pallas_call | solution.py:245
  21.9 7.6 %invert_classes_0.1.rest_4_.inverse_ref = f32[2,256,256]{2,1,0:T(8,128)S(1)} custom-call(s32[2]{0:T(128)S(1)} %fusion.counts_ref, s32[2,1024]{1,0:T(2,128)S(1)} %copy-done.1, s16[1616,128]{1,0:T(8,128)(2,1)S(1)} %sum_step_01.1.rest_0_.rest_1_), custom_call_target="tpu_custom_call" | custom-call | flops 1024 | bytes 1024 | tf_op jit(solution)/shard_map/invert_classes_0/pallas_call | solution.py:103
  29.6 2.2 %sum_step_02.1 = (s16[1616,128]{1,0:T(8,128)(2,1)S(1)}, bf16[128,2048]{1,0:T(8,128)(2,1)S(1)}) custom-call(s32[53]{0:T(128)S(1)} %fusion.1.table, s32[8]{0:T(128)S(1)} %pad_add_fusion.1.counts, s32[2,512]{1,0:T(2,128)S(1)} %pad_add_fusion.pairs_ref, bf16[128,32768]{1,0:T(8,128)(2,1)} %bitcast.15, bf16[128,2048]{1,0:T(8,128)(2,1)S(1)} %collective-permute-done.3.partner_ref, ...), custom_call_target="tpu_custom_call" | custom-call | flops 10000000000 | bytes 30000000 | tf_op jit(solution)/shard_map/sum_step_02/pallas_call | solution.py:245
  31.8 2.0 %collective-permute-start.10 = (s16[1616,128]{1,0:T(8,128)(2,1)S(1)}, s16[1616,128]{1,0:T(8,128)(2,1)S(1)}, u32[]{:S(2)}, u32[]{:S(2)}) collective-permute-start(s16[1616,128]{1,0:T(8,128)(2,1)S(1)} %get-tuple-element.27.rest_1_), channel_id=1, source_target_pairs={{0,8},{4,12},{8,0},{12,4},{16,24},{20,28},{24,16},{28,20},{1,9},{5... | collective-permute-start | bytes 1241096 | tf_op jit(solution)/shard_map/ppermute | solution.py:424
  33.8 2.3 %collective-permute-start.9 = (bf16[128,1024]{1,0:T(8,128)(2,1)S(1)}, bf16[128,1024]{1,0:T(8,128)(2,1)S(1)}, u32[]{:S(2)}, u32[]{:S(2)}) collective-permute-start(bf16[128,1024]{1,0:T(8,128)(2,1)S(1)} %collective-permute-done.6.rest_3_), channel_id=1, source_target_pairs={{0,4},{4,0},{8,12},{12,8},{16,20},{20,16},{24,28},{28,24},{1,5},{5... | collective-permute-start | bytes 786440 | tf_op jit(solution)/shard_map/ppermute | solution.py:429
  36.1 2.2 %sum_step_03.1 = (s16[1616,128]{1,0:T(8,128)(2,1)S(1)}, bf16[128,2048]{1,0:T(8,128)(2,1)S(1)}) custom-call(s32[53]{0:T(128)S(1)} %fusion.1.table, s32[8]{0:T(128)S(1)} %pad_add_fusion.1.counts, s32[2,512]{1,0:T(2,128)S(1)} %pad_add_fusion.pairs_ref, bf16[128,32768]{1,0:T(8,128)(2,1)} %bitcast.17, bf16[128,2048]{1,0:T(8,128)(2,1)S(1)} %collective-permute-done.3.partner_ref, ...), custom_call_target="tpu_custom_call" | custom-call | flops 10000000000 | bytes 30000000 | tf_op jit(solution)/shard_map/sum_step_03/pallas_call | solution.py:245
  38.5 1.9 %collective-permute-start.12 = (bf16[128,2048]{1,0:T(8,128)(2,1)S(1)}, bf16[128,2048]{1,0:T(8,128)(2,1)S(1)}, u32[]{:S(2)}, u32[]{:S(2)}) collective-permute-start(bf16[128,2048]{1,0:T(8,128)(2,1)S(1)} %get-tuple-element.30), channel_id=1, source_target_pairs={{0,4},{4,0},{8,12},{12,8},{16,20},{20,16},{24,28},{28,24},{1,5},{5... | collective-permute-start | bytes 1572872 | tf_op jit(solution)/shard_map/ppermute | solution.py:376
  40.4 2.9 %collective-permute-done.9.rest_1_ = bf16[128,1024]{1,0:T(8,128)(2,1)S(1)} collective-permute-done((bf16[128,1024]{1,0:T(8,128)(2,1)S(1)}, bf16[128,1024]{1,0:T(8,128)(2,1)S(1)}, u32[]{:S(2)}, u32[]{:S(2)}) %collective-permute-start.9) | collective-permute-done | bytes 262176 | tf_op jit(solution)/shard_map/ppermute | solution.py:429
  43.3 1.0 collective-permute-done.10.rest_3_.rest_0_.rest_1_
  44.3 10.2 %collective-permute-done.7.partner_ref = bf16[128,2048]{1,0:T(8,128)(2,1)S(1)} collective-permute-done((bf16[128,2048]{1,0:T(8,128)(2,1)S(1)}, bf16[128,2048]{1,0:T(8,128)(2,1)S(1)}, u32[]{:S(2)}, u32[]{:S(2)}) %collective-permute-start.7) | collective-permute-done | bytes 524320 | tf_op jit(solution)/shard_map/ppermute | solution.py:376
  54.5 2.0 %sum_step_04.1.rest_2_ = s16[1616,128]{1,0:T(8,128)(2,1)S(1)} custom-call(s32[53]{0:T(128)S(1)} %fusion.1.table, s32[8]{0:T(128)S(1)} %pad_add_fusion.1.counts, s32[2,512]{1,0:T(2,128)S(1)} %pad_add_fusion.pairs_ref, bf16[128,32768]{1,0:T(8,128)(2,1)} %bitcast.19, bf16[128,2048]{1,0:T(8,128)(2,1)S(1)} %collective-permute-done.7.partner_ref, ...), custom_call_target="tpu_custom_call" | custom-call | flops 10000000000 | bytes 30000000 | tf_op jit(solution)/shard_map/sum_step_04/pallas_call | solution.py:245
  57.3 4.6 %collective-permute-start.15 = (s16[1616,128]{1,0:T(8,128)(2,1)S(1)}, s16[1616,128]{1,0:T(8,128)(2,1)S(1)}, u32[]{:S(2)}, u32[]{:S(2)}) collective-permute-start(s16[1616,128]{1,0:T(8,128)(2,1)S(1)} %sum_step_04.1.rest_2_), channel_id=1, source_target_pairs={{0,8},{4,12},{24,16},{28,20},{1,9},{5,13},{25,17},{29,21},{2,10},{... | collective-permute-start | bytes 1241096 | tf_op jit(solution)/shard_map/ppermute | solution.py:424
  61.9 2.4 %sum_step_05.1 = (s16[1616,128]{1,0:T(8,128)(2,1)S(1)}, bf16[128,4096]{1,0:T(8,128)(2,1)S(1)}) custom-call(s32[53]{0:T(128)S(1)} %fusion.1.table, s32[8]{0:T(128)S(1)} %pad_add_fusion.1.counts, s32[2,512]{1,0:T(2,128)S(1)} %pad_add_fusion.pairs_ref, bf16[128,32768]{1,0:T(8,128)(2,1)} %bitcast.20, bf16[128,2048]{1,0:T(8,128)(2,1)S(1)} %collective-permute-done.7.partner_ref, ...), custom_call_target="tpu_custom_call" | custom-call | flops 10000000000 | bytes 30000000 | tf_op jit(solution)/shard_map/sum_step_05/pallas_call | solution.py:245
  65.1 4.4 %collective-permute-start.14 = (s16[1616,128]{1,0:T(8,128)(2,1)S(1)}, s16[1616,128]{1,0:T(8,128)(2,1)S(1)}, u32[]{:S(2)}, u32[]{:S(2)}) collective-permute-start(s16[1616,128]{1,0:T(8,128)(2,1)S(1)} %get-tuple-element.32.rest_1_), channel_id=1, source_target_pairs={{0,8},{4,12},{24,16},{28,20},{1,9},{5,13},{25,17},{29,21},{2,10},{... | collective-permute-start | bytes 1241096 | tf_op jit(solution)/shard_map/ppermute | solution.py:424
  69.4 1.7 %collective-permute-start.13 = (bf16[128,4096]{1,0:T(8,128)(2,1)S(1)}, bf16[128,4096]{1,0:T(8,128)(2,1)S(1)}, u32[]{:S(2)}, u32[]{:S(2)}) collective-permute-start(bf16[128,4096]{1,0:T(8,128)(2,1)S(1)} %get-tuple-element.31), channel_id=1, source_target_pairs={{0,4},{4,0},{8,12},{12,8},{16,20},{20,16},{24,28},{28,24},{1,5},{5... | collective-permute-start | bytes 3145736 | tf_op jit(solution)/shard_map/ppermute | solution.py:376
  71.1 2.0 %sum_step_06.1.rest_1_ = s16[1616,128]{1,0:T(8,128)(2,1)S(1)} custom-call(s32[53]{0:T(128)S(1)} %fusion.1.table, s32[8]{0:T(128)S(1)} %pad_add_fusion.1.counts, s32[2,512]{1,0:T(2,128)S(1)} %pad_add_fusion.pairs_ref, bf16[128,32768]{1,0:T(8,128)(2,1)} %bitcast.22, bf16[128,2048]{1,0:T(8,128)(2,1)S(1)} %collective-permute-done.12.rest_4_.partner_ref, ...), custom_call_target="tpu_custom_call" | custom-call | flops 10000000000 | bytes 30000000 | tf_op jit(solution)/shard_map/sum_step_06/pallas_call | solution.py:245
  73.8 3.3 %collective-permute-start.18 = (s16[1616,128]{1,0:T(8,128)(2,1)S(1)}, s16[1616,128]{1,0:T(8,128)(2,1)S(1)}, u32[]{:S(2)}, u32[]{:S(2)}) collective-permute-start(s16[1616,128]{1,0:T(8,128)(2,1)S(1)} %sum_step_06.1.rest_1_), channel_id=1, source_target_pairs={{0,8},{4,12},{24,16},{28,20},{1,9},{5,13},{25,17},{29,21},{2,10},{... | collective-permute-start | bytes 1241096 | tf_op jit(solution)/shard_map/ppermute | solution.py:424
  77.2 2.1 %collective-permute-done.14.rest_2_.rest_1_ = s16[1616,128]{1,0:T(8,128)(2,1)S(1)} collective-permute-done((s16[1616,128]{1,0:T(8,128)(2,1)S(1)}, s16[1616,128]{1,0:T(8,128)(2,1)S(1)}, u32[]{:S(2)}, u32[]{:S(2)}) %collective-permute-start.14) | collective-permute-done | bytes 413728 | tf_op jit(solution)/shard_map/ppermute | solution.py:424
  79.3 2.0 %sum_step_07.1.rest_2_ = s16[1616,128]{1,0:T(8,128)(2,1)S(1)} custom-call(s32[53]{0:T(128)S(1)} %fusion.1.table, s32[8]{0:T(128)S(1)} %pad_add_fusion.1.counts, s32[2,512]{1,0:T(2,128)S(1)} %pad_add_fusion.pairs_ref, bf16[128,32768]{1,0:T(8,128)(2,1)} %bitcast.23, bf16[128,2048]{1,0:T(8,128)(2,1)S(1)} %collective-permute-done.12.rest_4_.partner_ref, ...), custom_call_target="tpu_custom_call" | custom-call | flops 10000000000 | bytes 30000000 | tf_op jit(solution)/shard_map/sum_step_07/pallas_call | solution.py:245
  82.0 6.8 %collective-permute-start.20 = (s16[1616,128]{1,0:T(8,128)(2,1)S(1)}, s16[1616,128]{1,0:T(8,128)(2,1)S(1)}, u32[]{:S(2)}, u32[]{:S(2)}) collective-permute-start(s16[1616,128]{1,0:T(8,128)(2,1)S(1)} %sum_step_07.1.rest_2_), channel_id=1, source_target_pairs={{0,8},{4,12},{24,16},{28,20},{1,9},{5,13},{25,17},{29,21},{2,10},{... | collective-permute-start | bytes 1241096 | tf_op jit(solution)/shard_map/ppermute | solution.py:424
  88.8 2.3 %collective-permute-done.13.partner_ref = bf16[128,4096]{1,0:T(8,128)(2,1)S(1)} collective-permute-done((bf16[128,4096]{1,0:T(8,128)(2,1)S(1)}, bf16[128,4096]{1,0:T(8,128)(2,1)S(1)}, u32[]{:S(2)}, u32[]{:S(2)}) %collective-permute-start.13) | collective-permute-done | bytes 1048608 | tf_op jit(solution)/shard_map/ppermute | solution.py:376
  91.1 2.2 %sum_step_08.1 = (s16[1616,128]{1,0:T(8,128)(2,1)S(1)}, bf16[128,2048]{1,0:T(8,128)(2,1)S(1)}) custom-call(s32[53]{0:T(128)S(1)} %fusion.1.table, s32[8]{0:T(128)S(1)} %pad_add_fusion.1.counts, s32[2,512]{1,0:T(2,128)S(1)} %pad_add_fusion.pairs_ref, bf16[128,32768]{1,0:T(8,128)(2,1)} %bitcast.24, bf16[128,4096]{1,0:T(8,128)(2,1)S(1)} %collective-permute-done.13.partner_ref, ...), custom_call_target="tpu_custom_call" | custom-call | flops 10000000000 | bytes 30000000 | tf_op jit(solution)/shard_map/sum_step_08/pallas_call | solution.py:245
  93.4 1.3 %collective-permute-start.24 = (bf16[128,2048]{1,0:T(8,128)(2,1)S(1)}, bf16[128,2048]{1,0:T(8,128)(2,1)S(1)}, u32[]{:S(2)}, u32[]{:S(2)}) collective-permute-start(bf16[128,2048]{1,0:T(8,128)(2,1)S(1)} %get-tuple-element.36), channel_id=1, source_target_pairs={{0,4},{4,0},{8,12},{12,8},{16,20},{20,16},{24,28},{28,24},{1,5},{5... | collective-permute-start | bytes 1572872 | tf_op jit(solution)/shard_map/ppermute | solution.py:376
  94.7 4.0 %collective-permute-done.20.rest_3_.rest_0_ = s16[1616,128]{1,0:T(8,128)(2,1)S(1)} collective-permute-done((s16[1616,128]{1,0:T(8,128)(2,1)S(1)}, s16[1616,128]{1,0:T(8,128)(2,1)S(1)}, u32[]{:S(2)}, u32[]{:S(2)}) %collective-permute-start.20) | collective-permute-done | bytes 413728 | tf_op jit(solution)/shard_map/ppermute | solution.py:424
  98.7 2.2 %sum_step_09.1 = (s16[1616,128]{1,0:T(8,128)(2,1)S(1)}, bf16[128,2048]{1,0:T(8,128)(2,1)S(1)}) custom-call(s32[53]{0:T(128)S(1)} %fusion.1.table, s32[8]{0:T(128)S(1)} %pad_add_fusion.1.counts, s32[2,512]{1,0:T(2,128)S(1)} %pad_add_fusion.pairs_ref, bf16[128,32768]{1,0:T(8,128)(2,1)} %bitcast.26, bf16[128,4096]{1,0:T(8,128)(2,1)S(1)} %collective-permute-done.13.partner_ref, ...), custom_call_target="tpu_custom_call" | custom-call | flops 10000000000 | bytes 30000000 | tf_op jit(solution)/shard_map/sum_step_09/pallas_call | solution.py:245
  101.0 2.5 %collective-permute-start.25 = (s16[1616,128]{1,0:T(8,128)(2,1)S(1)}, s16[1616,128]{1,0:T(8,128)(2,1)S(1)}, u32[]{:S(2)}, u32[]{:S(2)}) collective-permute-start(s16[1616,128]{1,0:T(8,128)(2,1)S(1)} %get-tuple-element.35.rest_1_), channel_id=1, source_target_pairs={{0,8},{4,12},{8,24},{12,28},{16,0},{20,4},{24,16},{28,20},{1,9},{5... | collective-permute-start | bytes 1241096 | tf_op jit(solution)/shard_map/ppermute | solution.py:424
  103.5 1.4 %collective-permute-start.22 = (bf16[128,2048]{1,0:T(8,128)(2,1)S(1)}, bf16[128,2048]{1,0:T(8,128)(2,1)S(1)}, u32[]{:S(2)}, u32[]{:S(2)}) collective-permute-start(bf16[128,2048]{1,0:T(8,128)(2,1)S(1)} %get-tuple-element.34), channel_id=1, source_target_pairs={{0,4},{4,0},{8,12},{12,8},{16,20},{20,16},{24,28},{28,24},{1,5},{5... | collective-permute-start | bytes 1572872 | tf_op jit(solution)/shard_map/ppermute | solution.py:376
  104.9 2.7 %collective-permute-done.23.rest_2_.rest_4_.rest_5_ = s16[1616,128]{1,0:T(8,128)(2,1)S(1)} collective-permute-done((s16[1616,128]{1,0:T(8,128)(2,1)S(1)}, s16[1616,128]{1,0:T(8,128)(2,1)S(1)}, u32[]{:S(2)}, u32[]{:S(2)}) %collective-permute-start.23) | collective-permute-done | bytes 413728 | tf_op jit(solution)/shard_map/ppermute | solution.py:424
  107.6 0.7 collective-permute-done.24.rest_3_.partner_ref
  108.3 2.0 %sum_step_10.1.rest_1_ = s16[1616,128]{1,0:T(8,128)(2,1)S(1)} custom-call(s32[53]{0:T(128)S(1)} %fusion.1.table, s32[8]{0:T(128)S(1)} %pad_add_fusion.1.counts, s32[2,512]{1,0:T(2,128)S(1)} %pad_add_fusion.pairs_ref, bf16[128,32768]{1,0:T(8,128)(2,1)} %bitcast.28, bf16[128,4096]{1,0:T(8,128)(2,1)S(1)} %collective-permute-done.13.partner_ref, ...), custom_call_target="tpu_custom_call" | custom-call | flops 10000000000 | bytes 30000000 | tf_op jit(solution)/shard_map/sum_step_10/pallas_call | solution.py:245
  110.3 3.1 %collective-permute-start.27 = (s16[1616,128]{1,0:T(8,128)(2,1)S(1)}, s16[1616,128]{1,0:T(8,128)(2,1)S(1)}, u32[]{:S(2)}, u32[]{:S(2)}) collective-permute-start(s16[1616,128]{1,0:T(8,128)(2,1)S(1)} %sum_step_10.1.rest_1_), channel_id=1, source_target_pairs={{0,8},{4,12},{8,24},{12,28},{16,0},{20,4},{24,16},{28,20},{1,9},{5... | collective-permute-start | bytes 1241096 | tf_op jit(solution)/shard_map/ppermute | solution.py:424
  113.4 3.9 %finish_0.1 = (f32[200,4096]{1,0:T(8,128)}, f32[8,128]{1,0:T(8,128)S(1)}) custom-call(s32[53]{0:T(128)S(1)} %fusion.1.table, s32[8]{0:T(128)S(1)} %pad_add_fusion.1.counts, s32[2,512]{1,0:T(2,128)S(1)} %pad_add_fusion.pairs_ref, bf16[128,32768]{1,0:T(8,128)(2,1)} %bitcast.29, bf16[128,2048]{1,0:T(8,128)(2,1)S(1)} %collective-permute-done.24.rest_3_.partner_ref, ...), custom_call_target="tpu_custom_call" | custom-call | flops 1024 | bytes 1024 | tf_op jit(solution)/shard_map/finish_0/pallas_call | solution.py:327
  117.3 2.0 %sum_step_11.1 = s16[1616,128]{1,0:T(8,128)(2,1)S(1)} custom-call(s32[53]{0:T(128)S(1)} %fusion.1.table, s32[8]{0:T(128)S(1)} %pad_add_fusion.1.counts, s32[2,512]{1,0:T(2,128)S(1)} %pad_add_fusion.pairs_ref, bf16[128,32768]{1,0:T(8,128)(2,1)} %bitcast.30, bf16[128,4096]{1,0:T(8,128)(2,1)S(1)} %collective-permute-done.13.partner_ref, ...), custom_call_target="tpu_custom_call" | custom-call | flops 10000000000 | bytes 30000000 | tf_op jit(solution)/shard_map/sum_step_11/pallas_call | solution.py:245
  119.3 1.7 %collective-permute-start.26 = (s16[1616,128]{1,0:T(8,128)(2,1)S(1)}, s16[1616,128]{1,0:T(8,128)(2,1)S(1)}, u32[]{:S(2)}, u32[]{:S(2)}) collective-permute-start(s16[1616,128]{1,0:T(8,128)(2,1)S(1)} %sum_step_11.1), channel_id=1, source_target_pairs={{0,8},{4,12},{8,24},{12,28},{16,0},{20,4},{24,16},{28,20},{1,9},{5... | collective-permute-start | bytes 1241096 | tf_op jit(solution)/shard_map/ppermute | solution.py:424
  121.0 3.6 %finish_1.1.rest_6_ = f32[200,4096]{1,0:T(8,128)} custom-call(s32[53]{0:T(128)S(1)} %fusion.1.table, s32[8]{0:T(128)S(1)} %pad_add_fusion.1.counts, s32[2,512]{1,0:T(2,128)S(1)} %pad_add_fusion.pairs_ref, bf16[128,32768]{1,0:T(8,128)(2,1)} %bitcast.31, ...), custom_call_target="tpu_custom_call", output_to_operand_aliasing={{}: (12, {})} | custom-call | flops 1024 | bytes 1024 | tf_op jit(solution)/shard_map/finish_1/pallas_call | solution.py:327
  125.0 3.6 %finish_2.1.rest_6_ = f32[200,4096]{1,0:T(8,128)} custom-call(s32[53]{0:T(128)S(1)} %fusion.1.table, s32[8]{0:T(128)S(1)} %pad_add_fusion.1.counts, s32[2,512]{1,0:T(2,128)S(1)} %pad_add_fusion.pairs_ref, bf16[128,32768]{1,0:T(8,128)(2,1)} %bitcast.32, bf16[128,2048]{1,0:T(8,128)(2,1)S(1)} %collective-permute-done.22.partner_ref, ...), custom_call_target="tpu_custom_call", output_to_operand_aliasing={{}: (12, {})} | custom-call | flops 1024 | bytes 1024 | tf_op jit(solution)/shard_map/finish_2/pallas_call | solution.py:327
  128.6 0.9 collective-permute-done.26.rest_4_.rest_5_
  129.4 3.6 %finish_3.1 = f32[200,4096]{1,0:T(8,128)} custom-call(s32[53]{0:T(128)S(1)} %fusion.1.table, s32[8]{0:T(128)S(1)} %pad_add_fusion.1.counts, s32[2,512]{1,0:T(2,128)S(1)} %pad_add_fusion.pairs_ref, bf16[128,32768]{1,0:T(8,128)(2,1)} %bitcast.33, bf16[128,2048]{1,0:T(8,128)(2,1)S(1)} %collective-permute-done.22.partner_ref, ...), custom_call_target="tpu_custom_call", output_to_operand_aliasing={{}: (12, {})} | custom-call | flops 1024 | bytes 1024 | tf_op jit(solution)/shard_map/finish_3/pallas_call | solution.py:327
  (37 shorter events, 5.2 us)
Async XLA Ops:
  0.0 0.7 copy-start
  1.6 12.7 %collective-permute-start.2 = (s32[2]{0:T(128)S(1)}, s32[2]{0:T(128)S(1)}, u32[]{:S(2)}, u32[]{:S(2)}) collective-permute-start(s32[2]{0:T(128)S(1)} %fusion.counts_ref), channel_id=1, source_target_pairs={{0,24},{4,28},{8,0},{12,4},{16,8},{20,12},{24,16},{28,20},{1,25},{... | collective-permute-start | bytes 32 | tf_op jit(solution)/shard_map/ppermute | solution.py:392
  6.7 7.8 %collective-permute-start.1 = (s32[2]{0:T(128)S(1)}, s32[2]{0:T(128)S(1)}, u32[]{:S(2)}, u32[]{:S(2)}) collective-permute-start(s32[2]{0:T(128)S(1)} %fusion.counts_ref), channel_id=1, source_target_pairs={{0,16},{4,20},{8,24},{12,28},{16,0},{20,4},{24,8},{28,12},{1,17},{... | collective-permute-start | bytes 32 | tf_op jit(solution)/shard_map/ppermute | solution.py:392
  6.7 7.8 %collective-permute-start = (s32[2]{0:T(128)S(1)}, s32[2]{0:T(128)S(1)}, u32[]{:S(2)}, u32[]{:S(2)}) collective-permute-start(s32[2]{0:T(128)S(1)} %fusion.counts_ref), channel_id=1, source_target_pairs={{0,8},{4,12},{8,16},{12,20},{16,24},{20,28},{24,0},{28,4},{1,9},{5... | collective-permute-start | bytes 32 | tf_op jit(solution)/shard_map/ppermute | solution.py:392
  8.9 20.6 %collective-permute-start.6 = (bf16[128,1024]{1,0:T(8,128)(2,1)S(1)}, bf16[128,1024]{1,0:T(8,128)(2,1)S(1)}, u32[]{:S(2)}, u32[]{:S(2)}) collective-permute-start(bf16[128,1024]{1,0:T(8,128)(2,1)S(1)} %get-tuple-element.39), channel_id=1, source_target_pairs={{0,8},{4,12},{8,0},{12,4},{16,24},{20,28},{24,16},{28,20},{1,9},{5... | collective-permute-start | bytes 786440 | tf_op jit(solution)/shard_map/ppermute | solution.py:396
  11.4 8.4 %collective-permute-start.4 = (bf16[128,1024]{1,0:T(8,128)(2,1)S(1)}, bf16[128,1024]{1,0:T(8,128)(2,1)S(1)}, u32[]{:S(2)}, u32[]{:S(2)}) collective-permute-start(bf16[128,1024]{1,0:T(8,128)(2,1)S(1)} %get-tuple-element.40), channel_id=1, source_target_pairs={{0,4},{4,0},{8,12},{12,8},{16,20},{20,16},{24,28},{28,24},{1,5},{5... | collective-permute-start | bytes 786440 | tf_op jit(solution)/shard_map/ppermute | solution.py:376
  14.4 15.2 %collective-permute-start.5 = (bf16[128,1024]{1,0:T(8,128)(2,1)S(1)}, bf16[128,1024]{1,0:T(8,128)(2,1)S(1)}, u32[]{:S(2)}, u32[]{:S(2)}) collective-permute-start(bf16[128,1024]{1,0:T(8,128)(2,1)S(1)} %get-tuple-element.41), channel_id=1, source_target_pairs={{0,8},{4,12},{8,0},{12,4},{16,24},{20,28},{24,16},{28,20},{1,9},{5... | collective-permute-start | bytes 786440 | tf_op jit(solution)/shard_map/ppermute | solution.py:397
  15.7 13.9 %collective-permute-start.3 = (bf16[128,2048]{1,0:T(8,128)(2,1)S(1)}, bf16[128,2048]{1,0:T(8,128)(2,1)S(1)}, u32[]{:S(2)}, u32[]{:S(2)}) collective-permute-start(bf16[128,2048]{1,0:T(8,128)(2,1)S(1)} %dynamic-slice_bitcast_fusion), channel_id=1, source_target_pairs={{0,4},{4,0},{8,12},{12,8},{16,20},{20,16},{24,28},{28,24},{1,5},{5... | collective-permute-start | bytes 1572872 | tf_op jit(solution)/shard_map/ppermute | solution.py:376
  19.9 2.1 %copy-start.1 = (s32[2,1024]{1,0:T(2,128)S(1)}, s32[2,1024]{1,0:T(2,128)}, u32[]{:S(2)}) copy-start(s32[2,1024]{1,0:T(2,128)} %pairs_ref.1) | copy-start | bytes 24580
  21.9 14.3 %collective-permute-start.8 = (s16[1616,128]{1,0:T(8,128)(2,1)S(1)}, s16[1616,128]{1,0:T(8,128)(2,1)S(1)}, u32[]{:S(2)}, u32[]{:S(2)}) collective-permute-start(s16[1616,128]{1,0:T(8,128)(2,1)S(1)} %sum_step_01.1.rest_0_.rest_1_), channel_id=1, source_target_pairs={{0,8},{4,12},{8,0},{12,4},{16,24},{20,28},{24,16},{28,20},{1,9},{5... | collective-permute-start | bytes 1241096 | tf_op jit(solution)/shard_map/ppermute | solution.py:424
  31.8 12.6 %collective-permute-start.10 = (s16[1616,128]{1,0:T(8,128)(2,1)S(1)}, s16[1616,128]{1,0:T(8,128)(2,1)S(1)}, u32[]{:S(2)}, u32[]{:S(2)}) collective-permute-start(s16[1616,128]{1,0:T(8,128)(2,1)S(1)} %get-tuple-element.27.rest_1_), channel_id=1, source_target_pairs={{0,8},{4,12},{8,0},{12,4},{16,24},{20,28},{24,16},{28,20},{1,9},{5... | collective-permute-start | bytes 1241096 | tf_op jit(solution)/shard_map/ppermute | solution.py:424
  33.8 9.5 %collective-permute-start.9 = (bf16[128,1024]{1,0:T(8,128)(2,1)S(1)}, bf16[128,1024]{1,0:T(8,128)(2,1)S(1)}, u32[]{:S(2)}, u32[]{:S(2)}) collective-permute-start(bf16[128,1024]{1,0:T(8,128)(2,1)S(1)} %collective-permute-done.6.rest_3_), channel_id=1, source_target_pairs={{0,4},{4,0},{8,12},{12,8},{16,20},{20,16},{24,28},{28,24},{1,5},{5... | collective-permute-start | bytes 786440 | tf_op jit(solution)/shard_map/ppermute | solution.py:429
  36.1 18.5 %collective-permute-start.7 = (bf16[128,2048]{1,0:T(8,128)(2,1)S(1)}, bf16[128,2048]{1,0:T(8,128)(2,1)S(1)}, u32[]{:S(2)}, u32[]{:S(2)}) collective-permute-start(bf16[128,2048]{1,0:T(8,128)(2,1)S(1)} %get-tuple-element.26), channel_id=1, source_target_pairs={{0,4},{4,0},{8,12},{12,8},{16,20},{20,16},{24,28},{28,24},{1,5},{5... | collective-permute-start | bytes 1572872 | tf_op jit(solution)/shard_map/ppermute | solution.py:376
  38.3 23.6 %collective-permute-start.11 = (s16[1616,128]{1,0:T(8,128)(2,1)S(1)}, s16[1616,128]{1,0:T(8,128)(2,1)S(1)}, u32[]{:S(2)}, u32[]{:S(2)}) collective-permute-start(s16[1616,128]{1,0:T(8,128)(2,1)S(1)} %get-tuple-element.29.rest_2_), channel_id=1, source_target_pairs={{0,8},{4,12},{8,0},{12,4},{16,24},{20,28},{24,16},{28,20},{1,9},{5... | collective-permute-start | bytes 1241096 | tf_op jit(solution)/shard_map/ppermute | solution.py:424
  38.5 23.4 %collective-permute-start.12 = (bf16[128,2048]{1,0:T(8,128)(2,1)S(1)}, bf16[128,2048]{1,0:T(8,128)(2,1)S(1)}, u32[]{:S(2)}, u32[]{:S(2)}) collective-permute-start(bf16[128,2048]{1,0:T(8,128)(2,1)S(1)} %get-tuple-element.30), channel_id=1, source_target_pairs={{0,4},{4,0},{8,12},{12,8},{16,20},{20,16},{24,28},{28,24},{1,5},{5... | collective-permute-start | bytes 1572872 | tf_op jit(solution)/shard_map/ppermute | solution.py:376
  56.6 14.6 %collective-permute-start.16 = (s16[1616,128]{1,0:T(8,128)(2,1)S(1)}, s16[1616,128]{1,0:T(8,128)(2,1)S(1)}, u32[]{:S(2)}, u32[]{:S(2)}) collective-permute-start(s16[1616,128]{1,0:T(8,128)(2,1)S(1)} %sum_step_04.1.rest_2_), channel_id=1, source_target_pairs={{8,16},{12,20},{16,8},{20,12},{9,17},{13,21},{17,9},{21,13},{10,18... | collective-permute-start | bytes 1241096 | tf_op jit(solution)/shard_map/ppermute | solution.py:424
  57.3 13.9 %collective-permute-start.15 = (s16[1616,128]{1,0:T(8,128)(2,1)S(1)}, s16[1616,128]{1,0:T(8,128)(2,1)S(1)}, u32[]{:S(2)}, u32[]{:S(2)}) collective-permute-start(s16[1616,128]{1,0:T(8,128)(2,1)S(1)} %sum_step_04.1.rest_2_), channel_id=1, source_target_pairs={{0,8},{4,12},{24,16},{28,20},{1,9},{5,13},{25,17},{29,21},{2,10},{... | collective-permute-start | bytes 1241096 | tf_op jit(solution)/shard_map/ppermute | solution.py:424
  64.4 12.8 %collective-permute-start.17 = (s16[1616,128]{1,0:T(8,128)(2,1)S(1)}, s16[1616,128]{1,0:T(8,128)(2,1)S(1)}, u32[]{:S(2)}, u32[]{:S(2)}) collective-permute-start(s16[1616,128]{1,0:T(8,128)(2,1)S(1)} %get-tuple-element.32.rest_1_), channel_id=1, source_target_pairs={{8,16},{12,20},{16,8},{20,12},{9,17},{13,21},{17,9},{21,13},{10,18... | collective-permute-start | bytes 1241096 | tf_op jit(solution)/shard_map/ppermute | solution.py:424
  65.1 14.2 %collective-permute-start.14 = (s16[1616,128]{1,0:T(8,128)(2,1)S(1)}, s16[1616,128]{1,0:T(8,128)(2,1)S(1)}, u32[]{:S(2)}, u32[]{:S(2)}) collective-permute-start(s16[1616,128]{1,0:T(8,128)(2,1)S(1)} %get-tuple-element.32.rest_1_), channel_id=1, source_target_pairs={{0,8},{4,12},{24,16},{28,20},{1,9},{5,13},{25,17},{29,21},{2,10},{... | collective-permute-start | bytes 1241096 | tf_op jit(solution)/shard_map/ppermute | solution.py:424
  69.4 21.7 %collective-permute-start.13 = (bf16[128,4096]{1,0:T(8,128)(2,1)S(1)}, bf16[128,4096]{1,0:T(8,128)(2,1)S(1)}, u32[]{:S(2)}, u32[]{:S(2)}) collective-permute-start(bf16[128,4096]{1,0:T(8,128)(2,1)S(1)} %get-tuple-element.31), channel_id=1, source_target_pairs={{0,4},{4,0},{8,12},{12,8},{16,20},{20,16},{24,28},{28,24},{1,5},{5... | collective-permute-start | bytes 3145736 | tf_op jit(solution)/shard_map/ppermute | solution.py:376
  73.1 15.6 %collective-permute-start.19 = (s16[1616,128]{1,0:T(8,128)(2,1)S(1)}, s16[1616,128]{1,0:T(8,128)(2,1)S(1)}, u32[]{:S(2)}, u32[]{:S(2)}) collective-permute-start(s16[1616,128]{1,0:T(8,128)(2,1)S(1)} %sum_step_06.1.rest_1_), channel_id=1, source_target_pairs={{8,16},{12,20},{16,8},{20,12},{9,17},{13,21},{17,9},{21,13},{10,18... | collective-permute-start | bytes 1241096 | tf_op jit(solution)/shard_map/ppermute | solution.py:424
  73.8 14.9 %collective-permute-start.18 = (s16[1616,128]{1,0:T(8,128)(2,1)S(1)}, s16[1616,128]{1,0:T(8,128)(2,1)S(1)}, u32[]{:S(2)}, u32[]{:S(2)}) collective-permute-start(s16[1616,128]{1,0:T(8,128)(2,1)S(1)} %sum_step_06.1.rest_1_), channel_id=1, source_target_pairs={{0,8},{4,12},{24,16},{28,20},{1,9},{5,13},{25,17},{29,21},{2,10},{... | collective-permute-start | bytes 1241096 | tf_op jit(solution)/shard_map/ppermute | solution.py:424
  81.3 13.5 %collective-permute-start.21 = (s16[1616,128]{1,0:T(8,128)(2,1)S(1)}, s16[1616,128]{1,0:T(8,128)(2,1)S(1)}, u32[]{:S(2)}, u32[]{:S(2)}) collective-permute-start(s16[1616,128]{1,0:T(8,128)(2,1)S(1)} %sum_step_07.1.rest_2_), channel_id=1, source_target_pairs={{8,16},{12,20},{16,8},{20,12},{9,17},{13,21},{17,9},{21,13},{10,18... | collective-permute-start | bytes 1241096 | tf_op jit(solution)/shard_map/ppermute | solution.py:424
  82.0 16.8 %collective-permute-start.20 = (s16[1616,128]{1,0:T(8,128)(2,1)S(1)}, s16[1616,128]{1,0:T(8,128)(2,1)S(1)}, u32[]{:S(2)}, u32[]{:S(2)}) collective-permute-start(s16[1616,128]{1,0:T(8,128)(2,1)S(1)} %sum_step_07.1.rest_2_), channel_id=1, source_target_pairs={{0,8},{4,12},{24,16},{28,20},{1,9},{5,13},{25,17},{29,21},{2,10},{... | collective-permute-start | bytes 1241096 | tf_op jit(solution)/shard_map/ppermute | solution.py:424
  93.3 14.3 %collective-permute-start.23 = (s16[1616,128]{1,0:T(8,128)(2,1)S(1)}, s16[1616,128]{1,0:T(8,128)(2,1)S(1)}, u32[]{:S(2)}, u32[]{:S(2)}) collective-permute-start(s16[1616,128]{1,0:T(8,128)(2,1)S(1)} %get-tuple-element.33.rest_2_), channel_id=1, source_target_pairs={{0,8},{4,12},{8,24},{12,28},{16,0},{20,4},{24,16},{28,20},{1,9},{5... | collective-permute-start | bytes 1241096 | tf_op jit(solution)/shard_map/ppermute | solution.py:424
  93.4 14.9 %collective-permute-start.24 = (bf16[128,2048]{1,0:T(8,128)(2,1)S(1)}, bf16[128,2048]{1,0:T(8,128)(2,1)S(1)}, u32[]{:S(2)}, u32[]{:S(2)}) collective-permute-start(bf16[128,2048]{1,0:T(8,128)(2,1)S(1)} %get-tuple-element.36), channel_id=1, source_target_pairs={{0,4},{4,0},{8,12},{12,8},{16,20},{20,16},{24,28},{28,24},{1,5},{5... | collective-permute-start | bytes 1572872 | tf_op jit(solution)/shard_map/ppermute | solution.py:376
  101.0 16.3 %collective-permute-start.25 = (s16[1616,128]{1,0:T(8,128)(2,1)S(1)}, s16[1616,128]{1,0:T(8,128)(2,1)S(1)}, u32[]{:S(2)}, u32[]{:S(2)}) collective-permute-start(s16[1616,128]{1,0:T(8,128)(2,1)S(1)} %get-tuple-element.35.rest_1_), channel_id=1, source_target_pairs={{0,8},{4,12},{8,24},{12,28},{16,0},{20,4},{24,16},{28,20},{1,9},{5... | collective-permute-start | bytes 1241096 | tf_op jit(solution)/shard_map/ppermute | solution.py:424
  103.5 21.1 %collective-permute-start.22 = (bf16[128,2048]{1,0:T(8,128)(2,1)S(1)}, bf16[128,2048]{1,0:T(8,128)(2,1)S(1)}, u32[]{:S(2)}, u32[]{:S(2)}) collective-permute-start(bf16[128,2048]{1,0:T(8,128)(2,1)S(1)} %get-tuple-element.34), channel_id=1, source_target_pairs={{0,4},{4,0},{8,12},{12,8},{16,20},{20,16},{24,28},{28,24},{1,5},{5... | collective-permute-start | bytes 1572872 | tf_op jit(solution)/shard_map/ppermute | solution.py:376
  110.3 14.7 %collective-permute-start.27 = (s16[1616,128]{1,0:T(8,128)(2,1)S(1)}, s16[1616,128]{1,0:T(8,128)(2,1)S(1)}, u32[]{:S(2)}, u32[]{:S(2)}) collective-permute-start(s16[1616,128]{1,0:T(8,128)(2,1)S(1)} %sum_step_10.1.rest_1_), channel_id=1, source_target_pairs={{0,8},{4,12},{8,24},{12,28},{16,0},{20,4},{24,16},{28,20},{1,9},{5... | collective-permute-start | bytes 1241096 | tf_op jit(solution)/shard_map/ppermute | solution.py:424
  119.3 10.1 %collective-permute-start.26 = (s16[1616,128]{1,0:T(8,128)(2,1)S(1)}, s16[1616,128]{1,0:T(8,128)(2,1)S(1)}, u32[]{:S(2)}, u32[]{:S(2)}) collective-permute-start(s16[1616,128]{1,0:T(8,128)(2,1)S(1)} %sum_step_11.1), channel_id=1, source_target_pairs={{0,8},{4,12},{8,24},{12,28},{16,0},{20,4},{24,16},{28,20},{1,9},{5... | collective-permute-start | bytes 1241096 | tf_op jit(solution)/shard_map/ppermute | solution.py:424
